TPU v7x, 32 devices: a whole 2x2x4 slice. The times are simulated.
32 devices in a mesh: ctx: 16 (over z, y, x), fsdp: 2 (over core).
Axes of the slice: x: 2, y: 2, z: 4, core: 2. Of those that a mesh axis runs over, the one named last changes fastest.
Arguments:
- tokens: bfloat16 [2, 2048, 1024], P('fsdp', 'ctx'), may hold values from -6 to 6
- in_weight: bfloat16 [1024, 3072], P('fsdp'), may hold values from -0.1875 to 0.1875
- query_bias: bfloat16 [1024], P('fsdp'), may hold values from -3 to 3
- value_bias: bfloat16 [1024], P('fsdp'), may hold values from -0.23925781 to 0.23925781
- out_weight: bfloat16 [1024, 1024], P('fsdp'), may hold values from -2 to 2
- out_bias: bfloat16 [1024], P('fsdp'), may hold values from -1.1953125 to 1.1953125
- up_weight: bfloat16 [1024, 4096], P('fsdp'), may hold values from -0.1875 to 0.1875
- up_bias: bfloat16 [4096], P('fsdp'), may hold values from -1.796875 to 1.796875
- down_weight: bfloat16 [4096, 1024], P('fsdp'), may hold values from -0.125 to 0.125
- down_bias: bfloat16 [1024], P('fsdp'), may hold values from -2.390625 to 2.390625
- first_gain: bfloat16 [1024], P('fsdp'), may hold values from 0.5 to 1.5
- first_shift: bfloat16 [1024], P('fsdp'), may hold values from -1.1953125 to 1.1953125
- second_gain: bfloat16 [1024], P('fsdp'), may hold values from 0.5 to 1.5
- second_shift: bfloat16 [1024], P('fsdp'), may hold values from -1.1953125 to 1.1953125
- lengths: int32 [2, 2], P('fsdp'), may hold values from 1 to 1536, 2048 in all within a row
- slot_places: int32 [2, 2048], P('fsdp'), may hold values from 0 to 2047, each once within a row
- cotangent: bfloat16 [2, 2048, 1024], P('fsdp', 'ctx'), may hold values from -6 to 6
Outputs:
- layer_out: bfloat16 [2, 2048, 1024], P('fsdp', 'ctx')
- input_grad: bfloat16 [2, 2048, 1024], P('fsdp', 'ctx')
- in_weight_grad: float32 [1024, 3072], P(('ctx', 'fsdp'))
- query_bias_grad: float32 [1024], P(('ctx', 'fsdp'))
- value_bias_grad: float32 [1024], P(('ctx', 'fsdp'))
- out_weight_grad: float32 [1024, 1024], P(('ctx', 'fsdp'))
- out_bias_grad: float32 [1024], P(('ctx', 'fsdp'))
- up_weight_grad: float32 [1024, 4096], P(('ctx', 'fsdp'))
- up_bias_grad: float32 [4096], P(('ctx', 'fsdp'))
- down_weight_grad: float32 [4096, 1024], P(('ctx', 'fsdp'))
- down_bias_grad: float32 [1024], P(('ctx', 'fsdp'))
- first_gain_grad: float32 [1024], P(('ctx', 'fsdp'))
- first_shift_grad: float32 [1024], P(('ctx', 'fsdp'))
- second_gain_grad: float32 [1024], P(('ctx', 'fsdp'))
- second_shift_grad: float32 [1024], P(('ctx', 'fsdp'))
Inputs may be any that keep to these rules, and one draw needn't show every extreme that they name: In each batch 2 sequence lengths that sum to 2048; none is longer than 1536. `slot_places`: in each batch a permutation of the 2048 places: the place, in the batch's packed order, of the token held in each slot.
All inputs are finite; a program needn't handle non-finite values.
Results may differ from a plain program's by a relative error of at most 0.014.
Values may be sent and summed in bfloat16 or wider, within the bound.
A program may use at most 448 MiB of HBM per device.

v0:
```python
import jax
import jax.numpy as jnp
from jax import lax
from jax.sharding import PartitionSpec as P

H = 16
HD = 64


epsilon = 1e-05
far_below = -1e30


def normalize(values, gain, shift):
    center = values - jnp.mean(values, axis=-1, keepdims=True)
    spread = jnp.mean(center * center, axis=-1, keepdims=True)
    return center * lax.rsqrt(spread + epsilon) * gain + shift


def gelu_exact(values):
    return jax.nn.gelu(values, approximate=False)


def block_size(total):
    for size in range(min(2048, total), 0, -1):
        if total % size == 0:
            return size
    return total


def segment_of(places, starts):
    return jnp.sum((starts[None, :] <= places[:, None]).astype(jnp.int32), axis=1) - 1


def visible(query_place, query_segment, key_place, key_segment):
    return (key_segment[None, :] == query_segment[:, None]) & (
        key_place[None, :] <= query_place[:, None]
    )


def scores_of(queries, key_rows, allowed):
    scores = jnp.einsum("qhd,khd->hqk", queries, key_rows, preferred_element_type=jnp.float32)
    return jnp.where(allowed[None], scores, far_below)


def inner_rows(left, right):
    return jnp.einsum("tf,tg->fg", left, right, preferred_element_type=jnp.float32)


def times_transposed(left, right):
    return jnp.einsum("tg,fg->tf", left, right, preferred_element_type=jnp.float32)


def key_terms(probs_low, grad_scores, query_rows, grad_rows, size, width):
    grad_keys = jnp.einsum(
        "hqk,qhd->khd", grad_scores, query_rows, preferred_element_type=jnp.float32
    )
    grad_values = jnp.einsum(
        "hqk,qhd->khd", probs_low, grad_rows, preferred_element_type=jnp.float32
    )
    return jnp.concatenate(
        [grad_keys.reshape(size, width), grad_values.reshape(size, width)], axis=1
    )


def body(
    tokens,
    in_weight,
    query_bias,
    value_bias,
    out_weight,
    out_bias,
    up_weight,
    up_bias,
    down_weight,
    down_bias,
    first_gain,
    first_shift,
    second_gain,
    second_shift,
    lengths,
    slot_places,
    cotangent,
):
    gathered_params = (
        lax.all_gather(in_weight, "fsdp", axis=0, tiled=True),
        lax.all_gather(query_bias, "fsdp", axis=0, tiled=True),
        lax.all_gather(value_bias, "fsdp", axis=0, tiled=True),
        lax.all_gather(out_weight, "fsdp", axis=0, tiled=True),
        lax.all_gather(out_bias, "fsdp", axis=0, tiled=True),
        lax.all_gather(up_weight, "fsdp", axis=0, tiled=True),
        lax.all_gather(up_bias, "fsdp", axis=0, tiled=True),
        lax.all_gather(down_weight, "fsdp", axis=0, tiled=True),
        lax.all_gather(down_bias, "fsdp", axis=0, tiled=True),
        lax.all_gather(first_gain, "fsdp", axis=0, tiled=True),
        lax.all_gather(first_shift, "fsdp", axis=0, tiled=True),
        lax.all_gather(second_gain, "fsdp", axis=0, tiled=True),
        lax.all_gather(second_shift, "fsdp", axis=0, tiled=True),
    )
    (
        in_full,
        query_shift,
        value_shift,
        out_full,
        out_shift,
        up_full,
        up_shift,
        down_full,
        down_shift,
        gain_first,
        shift_first,
        gain_second,
        shift_second,
    ) = gathered_params
    query_shift = query_shift.astype(jnp.float32)
    value_shift = value_shift.astype(jnp.float32)
    out_shift = out_shift.astype(jnp.float32)
    up_shift = up_shift.astype(jnp.float32)
    down_shift = down_shift.astype(jnp.float32)
    gain_first = gain_first.astype(jnp.float32)
    shift_first = shift_first.astype(jnp.float32)
    gain_second = gain_second.astype(jnp.float32)
    shift_second = shift_second.astype(jnp.float32)
    inputs = tokens[0].astype(jnp.float32)
    rows = inputs.shape[0]
    width = inputs.shape[1]
    scale = HD ** (-0.5)
    places = slot_places[0]
    seq_lengths = lengths[0]
    starts = jnp.cumsum(seq_lengths) - seq_lengths
    key_segments = segment_of(places, starts)
    first_slot = lax.axis_index("ctx") * rows
    query_places = lax.dynamic_slice_in_dim(places, first_slot, rows)
    query_segments = lax.dynamic_slice_in_dim(key_segments, first_slot, rows)
    total_keys = places.shape[0]
    key_step = block_size(total_keys)
    block_count = total_keys // key_step
    place_blocks = places.reshape(block_count, key_step)
    segment_blocks = key_segments.reshape(block_count, key_step)
    normed_one = normalize(inputs, gain_first, shift_first).astype(jnp.bfloat16)
    projected = jnp.dot(normed_one, in_full, preferred_element_type=jnp.float32)
    queries = (
        ((projected[:, :width] + query_shift) * scale).astype(jnp.bfloat16).reshape(rows, H, HD)
    )
    key_value = jnp.concatenate(
        [projected[:, width : 2 * width], projected[:, 2 * width :] + value_shift], axis=1
    ).astype(jnp.bfloat16)
    gathered = lax.all_gather(key_value, "ctx", axis=0, tiled=True)
    pair_blocks = gathered.reshape(block_count, key_step, 2 * width)

    def split_pair(pair, size):
        return (pair[:, :width].reshape(size, H, HD), pair[:, width:].reshape(size, H, HD))

    def max_step(carry, block):
        top, total = carry
        pair, key_place, key_segment = block
        key_rows, value_rows = split_pair(pair, key_step)
        allowed = visible(query_places, query_segments, key_place, key_segment)
        scores = scores_of(queries, key_rows, allowed)
        new_top = jnp.maximum(top, jnp.max(scores, axis=2))
        expand = jnp.where(allowed[None], jnp.exp(scores - new_top[:, :, None]), 0.0)
        total = total * jnp.exp(top - new_top) + jnp.sum(expand, axis=2)
        return ((new_top, total), None)

    start_top = jnp.full((H, rows), far_below, jnp.float32)
    (top, total), unused = lax.scan(
        max_step,
        (start_top, jnp.zeros((H, rows), jnp.float32)),
        (pair_blocks, place_blocks, segment_blocks),
    )
    log_total = top + jnp.log(total)

    def value_step(summed, block):
        pair, key_place, key_segment = block
        key_rows, value_rows = split_pair(pair, key_step)
        allowed = visible(query_places, query_segments, key_place, key_segment)
        scores = scores_of(queries, key_rows, allowed)
        weights = jnp.where(allowed[None], jnp.exp(scores - log_total[:, :, None]), 0.0).astype(
            jnp.bfloat16
        )
        summed = summed + jnp.einsum(
            "hqk,khd->qhd", weights, value_rows, preferred_element_type=jnp.float32
        )
        return (summed, None)

    heads_out, unused = lax.scan(
        value_step,
        jnp.zeros((rows, H, HD), jnp.float32),
        (pair_blocks, place_blocks, segment_blocks),
    )
    attended = heads_out.reshape(rows, width).astype(jnp.bfloat16)
    middle = inputs + jnp.dot(attended, out_full, preferred_element_type=jnp.float32) + out_shift
    normed_two = normalize(middle, gain_second, shift_second).astype(jnp.bfloat16)
    hidden = jnp.dot(normed_two, up_full, preferred_element_type=jnp.float32) + up_shift
    active_full, gelu_back = jax.vjp(gelu_exact, hidden)
    active = active_full.astype(jnp.bfloat16)
    result = middle + jnp.dot(active, down_full, preferred_element_type=jnp.float32) + down_shift
    layer_out = result.astype(jnp.bfloat16)[None]
    grad_low = cotangent[0]
    grad_result = grad_low.astype(jnp.float32)
    down_grad = inner_rows(active, grad_low)
    down_bias_grad = jnp.sum(grad_result, axis=0)
    grad_active = times_transposed(grad_low, down_full)
    grad_hidden = gelu_back(grad_active)[0].astype(jnp.bfloat16)
    up_grad = inner_rows(normed_two, grad_hidden)
    up_bias_grad = jnp.sum(grad_hidden.astype(jnp.float32), axis=0)
    grad_normed_two = times_transposed(grad_hidden, up_full)
    unused, second_back = jax.vjp(normalize, middle, gain_second, shift_second)
    grad_middle_norm, gain_two_grad, shift_two_grad = second_back(grad_normed_two)
    grad_middle = grad_result + grad_middle_norm
    grad_branch = grad_middle.astype(jnp.bfloat16)
    out_grad = inner_rows(attended, grad_branch)
    out_bias_grad = jnp.sum(grad_branch.astype(jnp.float32), axis=0)
    grad_attended = (
        times_transposed(grad_branch, out_full).astype(jnp.bfloat16).reshape(rows, H, HD)
    )
    deltas = jnp.sum(grad_attended.astype(jnp.float32) * heads_out, axis=2).T

    def block_back(key_rows, value_rows, allowed):
        scores = scores_of(queries, key_rows, allowed)
        probs = jnp.where(allowed[None], jnp.exp(scores - log_total[:, :, None]), 0.0)
        grad_probs = jnp.einsum(
            "qhd,khd->hqk", grad_attended, value_rows, preferred_element_type=jnp.float32
        )
        grad_scores = (probs * (grad_probs - deltas[:, :, None])).astype(jnp.bfloat16)
        return (probs.astype(jnp.bfloat16), grad_scores)

    def query_term(grad_scores, key_rows):
        return jnp.einsum("hqk,khd->qhd", grad_scores, key_rows, preferred_element_type=jnp.float32)

    def whole_step(grad_queries, block):
        pair, key_place, key_segment = block
        key_rows, value_rows = split_pair(pair, key_step)
        allowed = visible(query_places, query_segments, key_place, key_segment)
        probs_low, grad_scores = block_back(key_rows, value_rows, allowed)
        grad_queries = grad_queries + query_term(grad_scores, key_rows)
        return (
            grad_queries,
            key_terms(probs_low, grad_scores, queries, grad_attended, key_step, width),
        )

    grad_queries, terms = lax.scan(
        whole_step,
        jnp.zeros((rows, H, HD), jnp.float32),
        (pair_blocks, place_blocks, segment_blocks),
    )
    key_grads = lax.psum_scatter(
        terms.reshape(total_keys, 2 * width), "ctx", scatter_dimension=0, tiled=True
    )
    key_grads_low = key_grads.astype(jnp.bfloat16)
    grad_queries_low = grad_queries.reshape(rows, width).astype(jnp.bfloat16)
    grad_projected = jnp.concatenate([grad_queries_low, key_grads_low], axis=1)
    in_grad_raw = inner_rows(normed_one, grad_projected)
    in_grad = jnp.concatenate([in_grad_raw[:, :width] * scale, in_grad_raw[:, width:]], axis=1)
    query_bias_grad = jnp.sum(grad_queries_low.astype(jnp.float32), axis=0) * scale
    value_bias_grad = jnp.sum(key_grads_low[:, width:].astype(jnp.float32), axis=0)
    grad_normed_one = times_transposed(
        grad_queries_low, in_full[:, :width]
    ) * scale + times_transposed(key_grads_low, in_full[:, width:])
    unused, first_back = jax.vjp(normalize, inputs, gain_first, shift_first)
    grad_inputs_norm, gain_one_grad, shift_one_grad = first_back(grad_normed_one)
    input_grad = (grad_middle + grad_inputs_norm).astype(jnp.bfloat16)[None]
    grads = (
        in_grad,
        query_bias_grad,
        value_bias_grad,
        out_grad,
        out_bias_grad,
        up_grad,
        up_bias_grad,
        down_grad,
        down_bias_grad,
        gain_one_grad,
        shift_one_grad,
        gain_two_grad,
        shift_two_grad,
    )
    summed = (
        lax.psum_scatter(grads[0], ("ctx", "fsdp"), scatter_dimension=0, tiled=True),
        lax.psum_scatter(grads[1], ("ctx", "fsdp"), scatter_dimension=0, tiled=True),
        lax.psum_scatter(grads[2], ("ctx", "fsdp"), scatter_dimension=0, tiled=True),
        lax.psum_scatter(grads[3], ("ctx", "fsdp"), scatter_dimension=0, tiled=True),
        lax.psum_scatter(grads[4], ("ctx", "fsdp"), scatter_dimension=0, tiled=True),
        lax.psum_scatter(grads[5], ("ctx", "fsdp"), scatter_dimension=0, tiled=True),
        lax.psum_scatter(grads[6], ("ctx", "fsdp"), scatter_dimension=0, tiled=True),
        lax.psum_scatter(grads[7], ("ctx", "fsdp"), scatter_dimension=0, tiled=True),
        lax.psum_scatter(grads[8], ("ctx", "fsdp"), scatter_dimension=0, tiled=True),
        lax.psum_scatter(grads[9], ("ctx", "fsdp"), scatter_dimension=0, tiled=True),
        lax.psum_scatter(grads[10], ("ctx", "fsdp"), scatter_dimension=0, tiled=True),
        lax.psum_scatter(grads[11], ("ctx", "fsdp"), scatter_dimension=0, tiled=True),
        lax.psum_scatter(grads[12], ("ctx", "fsdp"), scatter_dimension=0, tiled=True),
    )
    (
        in_weight_grad,
        query_bias_grad_out,
        value_bias_grad_out,
        out_weight_grad,
        out_bias_grad_out,
        up_weight_grad,
        up_bias_grad_out,
        down_weight_grad,
        down_bias_grad_out,
        first_gain_grad,
        first_shift_grad,
        second_gain_grad,
        second_shift_grad,
    ) = summed
    return (
        layer_out,
        input_grad,
        in_weight_grad,
        query_bias_grad_out,
        value_bias_grad_out,
        out_weight_grad,
        out_bias_grad_out,
        up_weight_grad,
        up_bias_grad_out,
        down_weight_grad,
        down_bias_grad_out,
        first_gain_grad,
        first_shift_grad,
        second_gain_grad,
        second_shift_grad,
    )


def solution(mesh):
    placed = (
        P("fsdp", "ctx", None),
        P("fsdp", None),
        P("fsdp"),
        P("fsdp"),
        P("fsdp", None),
        P("fsdp"),
        P("fsdp", None),
        P("fsdp"),
        P("fsdp", None),
        P("fsdp"),
        P("fsdp"),
        P("fsdp"),
        P("fsdp"),
        P("fsdp"),
        P("fsdp", None),
        P("fsdp", None),
        P("fsdp", "ctx", None),
    )
    return jax.shard_map(
        body,
        mesh=mesh,
        in_specs=placed,
        out_specs=(
            P("fsdp", "ctx", None),
            P("fsdp", "ctx", None),
            P(("ctx", "fsdp"), None),
            P(("ctx", "fsdp")),
            P(("ctx", "fsdp")),
            P(("ctx", "fsdp"), None),
            P(("ctx", "fsdp")),
            P(("ctx", "fsdp"), None),
            P(("ctx", "fsdp")),
            P(("ctx", "fsdp"), None),
            P(("ctx", "fsdp")),
            P(("ctx", "fsdp")),
            P(("ctx", "fsdp")),
            P(("ctx", "fsdp")),
            P(("ctx", "fsdp")),
        ),
        check_vma=False,
    )
```

profile of v0, /device:TPU:0, one launch (start us, length us, event | category | flops | bytes accessed | tf_op | source)
XLA Modules:
  0.0 1292.5 jit_solution(16775113669987074428)
XLA Ops:
  8.0 1.9 all-gather.3
  10.0 1.8 all-gather.2
  11.8 1.8 all-gather
  13.6 1.8 all-gather.1
  15.8 13.3 %all-gather.14.cloned.1.call-done = bf16[1024,3072]{1,0:T(8,128)(2,1)} async-done(((bf16[512,3072]{1,0:T(8,128)(2,1)}), bf16[1024,3072]{1,0:T(8,128)(2,1)}) %all-gather.14.cloned.1.call-update) | async-done | bytes 6291472 | tf_op jit(solution)/shard_map/all_gather | solution.py:86
  29.1 3.9 fusion.60
  36.2 1.8 all-gather.4
  38.0 1.8 all-gather.5
  39.8 1.8 all-gather.6
  41.6 1.8 all_gather.53
  44.1 104.1 %all-gather.16.cloned.1.call-done = bf16[2048,2048]{1,0:T(8,128)(2,1)} async-done(((bf16[128,2048]{1,0:T(8,128)(2,1)}), bf16[2048,2048]{1,0:T(8,128)(2,1)}) %all-gather.16.cloned.1.call-update) | async-done | bytes 8388624 | tf_op jit(solution)/shard_map/all_gather | solution.py:148
  148.2 6.3 fusion.67
  154.4 6.7 copy.49
  161.1 6.5 copy.47
  167.6 5.5 select_reduce_fusion.1
  173.1 4.6 select_reduce_fusion
  177.7 2.6 copy-done
  180.4 8.7 fusion.68
  189.1 2.5 fusion.69
  191.9 7.6 convolution_add_fusion
  199.5 3.9 all-gather.22.cloned.1.call-done
  203.4 10.4 convert_reduce_fusion
  213.9 3.1 multiply_reduce_fusion
  218.5 1.6 convolution_convert_fusion.1
  222.3 10.0 fusion.48
  232.4 10.4 multiply_convert_fusion
  244.0 3.0 copy-done.1
  247.0 2.2 copy-done.3
  249.2 6.3 pad_maximum_fusion
  256.5 2.8 fusion.71
  260.2 11.1 fusion.42
  271.4 8.2 fusion.63
  279.7 7.8 convert_reduce_fusion.5
  287.5 315.8 %reduce-scatter.6.cloned.1.call-done = f32[128,2048]{0,1:T(8,128)} async-done(((f32[2048,2048]{0,1:T(8,128)}), f32[128,2048]{0,1:T(8,128)}) %reduce-scatter.6.cloned.1.call-update) | async-done | bytes 1048592 | tf_op jit(solution)/shard_map/reduce_scatter | solution.py:247
  603.3 1.3 convert_element_type.143
  604.6 2.0 fusion.21
  606.5 3.8 slice.57
  610.3 2.4 slice_multiply_fusion
  612.7 10.7 pad_maximum_fusion.1
  624.1 2.0 all-gather.7
  626.1 10.1 fusion.20
  636.4 3.7 fusion.1
  640.1 2.5 fusion.64
  644.1 45.9 %all-reduce.9 = (f32[1024]{0:T(1024)S(1)}, f32[1024]{0:T(1024)S(1)}, f32[1024]{0:T(1024)S(1)}, f32[4096]{0:T(1024)S(1)}, f32[1024]{0:T(1024)S(1)}, /*index=5*/f3...) all-reduce(f32[1024]{0:T(1024)S(1)} %mul.227, ...), channel_id=4, replica_groups=mesh['ctx'=16,'fsdp'=2] {'ctx','fsdp'}, use_global_device_ids=true, to_apply=%region_16.17.clone | all-reduce | flops 12288 | bytes 98304
  695.2 57.6 %reduce-scatter.10.cloned.1.call-done = f32[32,1024]{1,0:T(8,128)} async-done(((f32[1024,1024]{1,0:T(8,128)}), f32[32,1024]{1,0:T(8,128)}) %reduce-scatter.10.cloned.1.call-update) | async-done | bytes 131088 | tf_op jit(solution)/shard_map/reduce_scatter | solution.py:282
  752.8 181.6 %reduce-scatter.14.cloned.1.call-done = f32[128,1024]{1,0:T(8,128)} async-done(((f32[4096,1024]{1,0:T(8,128)}), f32[128,1024]{1,0:T(8,128)}) %reduce-scatter.14.cloned.1.call-update) | async-done | bytes 524304 | tf_op jit(solution)/shard_map/reduce_scatter | solution.py:286
  934.4 187.4 %reduce-scatter.12.cloned.1.call-done = f32[32,4096]{1,0:T(8,128)} async-done(((f32[1024,4096]{1,0:T(8,128)}), f32[32,4096]{1,0:T(8,128)}) %reduce-scatter.12.cloned.1.call-update) | async-done | bytes 524304 | tf_op jit(solution)/shard_map/reduce_scatter | solution.py:284
  1121.8 163.7 %reduce-scatter.8.cloned.1.call-done = f32[32,3072]{1,0:T(8,128)} async-done(((f32[1024,3072]{1,0:T(8,128)}), f32[32,3072]{1,0:T(8,128)}) %reduce-scatter.8.cloned.1.call-update) | async-done | bytes 393232 | tf_op jit(solution)/shard_map/reduce_scatter | solution.py:279
  (127 shorter events, 19.8 us)
Async XLA Ops:
  7.2 0.8 copy-start.13
  7.2 2.8 copy-start.14
  7.2 4.6 copy-start.15
  7.2 6.4 copy-start.16
  7.2 8.2 copy-start.4
  7.2 21.9 %all-gather.14.cloned.1.call-start = ((), (), s32[]{:S(2)}) async-start(), calls=%async_computation.5 | async-start | bytes 9437184 | tf_op jit(solution)/shard_map/all_gather | solution.py:86
  8.0 140.2 %all-gather.16.cloned.1.call-start = ((), (), s32[]{:S(2)}) async-start(), calls=%async_computation.6 | async-start | bytes 8912896 | tf_op jit(solution)/shard_map/all_gather | solution.py:148
  15.7 17.2 %copy-start.21 = (f32[128]{0:T(128)}, f32[128]{0:T(128)S(1)}, u32[]{:S(2)}) copy-start(f32[128]{0:T(128)S(1)} %fusion.35) | copy-start | bytes 1540
  34.0 155.1 %all-gather.18.cloned.1.call-start = ((), (), s32[]{:S(2)}) async-start(), calls=%async_computation.7 | async-start | bytes 3145728 | tf_op jit(solution)/shard_map/all_gather | solution.py:89
  34.7 157.1 %all-gather.20.cloned.1.call-start = ((), (), s32[]{:S(2)}) async-start(), calls=%async_computation.8 | async-start | bytes 12582912 | tf_op jit(solution)/shard_map/all_gather | solution.py:91
  35.3 0.7 copy-start.23
  35.3 0.9 copy-start.17
  35.3 2.7 copy-start.18
  35.3 4.5 copy-start.19
  35.4 6.3 copy-start.12
  35.4 8.1 copy-start.11
  35.4 168.0 %all-gather.22.cloned.1.call-start = ((), (), s32[]{:S(2)}) async-start(), calls=%async_computation.9 | async-start | bytes 12582912 | tf_op jit(solution)/shard_map/all_gather | solution.py:93
  36.0 567.3 %reduce-scatter.6.cloned.1.call-start = ((), (), s32[]{:S(2)}) async-start(), calls=%async_computation.10 | async-start | bytes 17825792 | tf_op jit(solution)/shard_map/reduce_scatter | solution.py:247
  173.1 7.3 copy-start
  173.1 7.3 copy-start.6
  189.1 10.4 copy-start.9
  191.9 11.5 copy-start.7
  203.4 10.4 copy-start.2
  216.9 1.6 copy-start.5
  242.8 4.3 copy-start.1
  242.8 6.4 copy-start.3
  255.5 0.9 copy-start.10
  255.5 497.3 %reduce-scatter.10.cloned.1.call-start = ((), (), s32[]{:S(2)}) async-start(), calls=%async_computation.12 | async-start | bytes 4325376 | tf_op jit(solution)/shard_map/reduce_scatter | solution.py:282
  259.3 0.9 copy-start.8
  259.3 675.1 %reduce-scatter.14.cloned.1.call-start = ((), (), s32[]{:S(2)}) async-start(), calls=%async_computation.14 | async-start | bytes 17301504 | tf_op jit(solution)/shard_map/reduce_scatter | solution.py:286
  271.4 850.4 %reduce-scatter.12.cloned.1.call-start = ((), (), s32[]{:S(2)}) async-start(), calls=%async_computation.13 | async-start | bytes 17301504 | tf_op jit(solution)/shard_map/reduce_scatter | solution.py:284
  279.6 1005.8 %reduce-scatter.8.cloned.1.call-start = ((), (), s32[]{:S(2)}) async-start(), calls=%async_computation.11 | async-start | bytes 12976128 | tf_op jit(solution)/shard_map/reduce_scatter | solution.py:279
  623.4 0.7 copy-start.20
  640.1 2.6 copy-start.22
Sparse Core Ops, SparseCore 0:
  9.6 19.4 all-gather.13
  34.1 113.9 all-gather.15
  149.7 8.7 all-gather.17
  159.9 21.0 all-gather.19
  182.3 21.0 all-gather.21
  255.7 347.5 reduce-scatter.5
  606.1 146.6 reduce-scatter.9
  755.7 178.6 reduce-scatter.13
  937.3 184.4 reduce-scatter.11
  1128.2 157.1 reduce-scatter.7
where the time goes:
time: 1300 us; the launch traced here: 1290 us
  waiting for transfers between devices  1030 us (79%)
  matrix products  113 us (9%)
  blocking collectives  62.3 us (5%)
  local copies, waits for them, and re-layouts  41.4 us (3%)
  other arithmetic  30.5 us (2%)
  between operations  14.9 us (1%)
    reduce_scatter x1, waiting for transfers between devices, body(): lax.psum_scatter(terms.reshape(total_keys, 2 * width), 'ctx', scatter_dim...  316 us
    reduce_scatter x1, waiting for transfers between devices, body(): lax.psum_scatter(grads[5], ('ctx', 'fsdp'), scatter_dimension=0, tiled=True)  187 us
    reduce_scatter x1, waiting for transfers between devices, body(): lax.psum_scatter(grads[7], ('ctx', 'fsdp'), scatter_dimension=0, tiled=True)  182 us
    reduce_scatter x1, waiting for transfers between devices, body(): lax.psum_scatter(grads[0], ('ctx', 'fsdp'), scatter_dimension=0, tiled=True)  164 us
    all_gather x1, waiting for transfers between devices, body(): gathered = lax.all_gather(key_value, 'ctx', axis=0, tiled=True)  104 us
    reduce_scatter x1, waiting for transfers between devices, body(): lax.psum_scatter(grads[3], ('ctx', 'fsdp'), scatter_dimension=0, tiled=True)  57.6 us
    unnamed x1, blocking collectives  45.9 us
  transfers between devices with their start and end apart: 10, of which 8 were waited for; matrix products, arithmetic and copies ran while one was open for 10% of the time, Pallas kernels for 0%

commit v1 on v0

--- a/solution.py
+++ b/solution.py
@@ -63,7 +63,7 @@
     )
 
 
-def body(
+def body_general(
     tokens,
     in_weight,
     query_bias,
@@ -324,6 +324,172 @@
     )
 
 
+def body_heads(
+    tokens,
+    in_weight,
+    query_bias,
+    value_bias,
+    out_weight,
+    out_bias,
+    up_weight,
+    up_bias,
+    down_weight,
+    down_bias,
+    first_gain,
+    first_shift,
+    second_gain,
+    second_shift,
+    lengths,
+    slot_places,
+    cotangent,
+):
+    low = jnp.bfloat16
+    vectors = [
+        query_bias,
+        value_bias,
+        out_bias,
+        down_bias,
+        first_gain,
+        first_shift,
+        second_gain,
+        second_shift,
+    ]
+    half = query_bias.shape[0]
+    packed = jnp.concatenate(vectors + [up_bias]).reshape(-1, half)
+    packed = lax.all_gather(packed, "fsdp", axis=0).astype(jnp.float32)
+    pieces = jnp.concatenate([packed[0], packed[1]], axis=1)
+    (query_shift, value_shift, out_shift, down_shift) = (pieces[i] for i in range(4))
+    (gain_first, shift_first, gain_second, shift_second) = (pieces[i] for i in range(4, 8))
+    up_shift = packed[:, 8:].reshape(-1)
+    in_full = lax.all_gather(in_weight, "fsdp", axis=0, tiled=True)
+    out_full = lax.all_gather(out_weight, "fsdp", axis=0, tiled=True)
+    up_full = lax.all_gather(up_weight, "fsdp", axis=0, tiled=True)
+    down_full = lax.all_gather(down_weight, "fsdp", axis=0, tiled=True)
+    inputs = tokens[0].astype(jnp.float32)
+    rows, width = inputs.shape
+    scale = HD ** (-0.5)
+    places = slot_places[0]
+    starts = jnp.cumsum(lengths[0]) - lengths[0]
+    segments = segment_of(places, starts)
+    allowed = visible(places, segments, places, segments)
+    normed_one = normalize(inputs, gain_first, shift_first).astype(low)
+    projected = jnp.dot(normed_one, in_full, preferred_element_type=jnp.float32)
+    triple = jnp.concatenate(
+        [
+            (projected[:, :width] + query_shift) * scale,
+            projected[:, width : 2 * width],
+            projected[:, 2 * width :] + value_shift,
+        ],
+        axis=1,
+    ).astype(low)
+
+    def to_heads(rows_in, count):
+        parts = rows_in.reshape(rows, count, H, HD)
+        out = lax.all_to_all(parts, "ctx", split_axis=2, concat_axis=0, tiled=True)
+        return out.reshape(-1, count, HD)
+
+    def to_tokens(heads_in, count):
+        parts = heads_in.reshape(-1, count, 1, HD)
+        out = lax.all_to_all(parts, "ctx", split_axis=0, concat_axis=2, tiled=True)
+        return out.reshape(rows, count * width)
+
+    head = to_heads(triple, 3)
+    queries, key_rows, value_rows = head[:, 0], head[:, 1], head[:, 2]
+    scores = jnp.where(allowed, times_transposed(queries, key_rows), far_below)
+    top = jnp.max(scores, axis=1, keepdims=True)
+    total = jnp.sum(jnp.where(allowed, jnp.exp(scores - top), 0.0), axis=1, keepdims=True)
+    probs = jnp.where(allowed, jnp.exp(scores - (top + jnp.log(total))), 0.0)
+    probs_low = probs.astype(low)
+    head_out = jnp.dot(probs_low, value_rows, preferred_element_type=jnp.float32)
+    attended = to_tokens(head_out.astype(low), 1)
+    middle = inputs + jnp.dot(attended, out_full, preferred_element_type=jnp.float32) + out_shift
+    normed_two = normalize(middle, gain_second, shift_second).astype(low)
+    hidden = jnp.dot(normed_two, up_full, preferred_element_type=jnp.float32) + up_shift
+    active_full, gelu_back = jax.vjp(gelu_exact, hidden)
+    active = active_full.astype(low)
+    result = middle + jnp.dot(active, down_full, preferred_element_type=jnp.float32) + down_shift
+    layer_out = result.astype(low)[None]
+    grad_low = cotangent[0]
+    grad_result = grad_low.astype(jnp.float32)
+
+    def scattered(grad):
+        return lax.psum_scatter(
+            grad.astype(low), ("ctx", "fsdp"), scatter_dimension=0, tiled=True
+        ).astype(jnp.float32)
+
+    down_grad = scattered(inner_rows(active, grad_low))
+    down_bias_grad = jnp.sum(grad_result, axis=0)
+    grad_active = times_transposed(grad_low, down_full)
+    grad_hidden = gelu_back(grad_active)[0].astype(low)
+    up_grad = scattered(inner_rows(normed_two, grad_hidden))
+    up_bias_grad = jnp.sum(grad_hidden.astype(jnp.float32), axis=0)
+    grad_normed_two = times_transposed(grad_hidden, up_full)
+    unused, second_back = jax.vjp(normalize, middle, gain_second, shift_second)
+    grad_middle_norm, gain_two_grad, shift_two_grad = second_back(grad_normed_two)
+    grad_middle = grad_result + grad_middle_norm
+    grad_branch = grad_middle.astype(low)
+    out_grad = scattered(inner_rows(attended, grad_branch))
+    out_bias_grad = jnp.sum(grad_branch.astype(jnp.float32), axis=0)
+    grad_out = to_heads(times_transposed(grad_branch, out_full).astype(low), 1)[:, 0]
+    deltas = jnp.sum(grad_out.astype(jnp.float32) * head_out, axis=1, keepdims=True)
+    grad_probs = times_transposed(grad_out, value_rows)
+    grad_scores = (probs * (grad_probs - deltas)).astype(low)
+    grad_head = jnp.stack(
+        [
+            jnp.dot(grad_scores, key_rows, preferred_element_type=jnp.float32),
+            inner_rows(grad_scores, queries),
+            inner_rows(probs_low, grad_out),
+        ],
+        axis=1,
+    ).astype(low)
+    grad_projected = to_tokens(grad_head, 3)
+    in_raw = inner_rows(normed_one, grad_projected)
+    in_grad = scattered(jnp.concatenate([in_raw[:, :width] * scale, in_raw[:, width:]], axis=1))
+    bias_sums = jnp.sum(grad_projected.astype(jnp.float32), axis=0)
+    grad_normed_one = times_transposed(
+        grad_projected[:, :width], in_full[:, :width]
+    ) * scale + times_transposed(grad_projected[:, width:], in_full[:, width:])
+    unused, first_back = jax.vjp(normalize, inputs, gain_first, shift_first)
+    grad_inputs_norm, gain_one_grad, shift_one_grad = first_back(grad_normed_one)
+    input_grad = (grad_middle + grad_inputs_norm).astype(low)[None]
+    count = lax.axis_size("ctx") * lax.axis_size("fsdp")
+    small = (
+        bias_sums[:width] * scale,
+        bias_sums[2 * width :],
+        out_bias_grad,
+        up_bias_grad,
+        down_bias_grad,
+        gain_one_grad,
+        shift_one_grad,
+        gain_two_grad,
+        shift_two_grad,
+    )
+    split = jnp.concatenate([one.reshape(count, -1) for one in small], axis=1)
+    summed = lax.psum_scatter(split, ("ctx", "fsdp"), scatter_dimension=0, tiled=True)[0]
+    parts, at = [], 0
+    for one in small:
+        size = one.shape[0] // count
+        parts.append(summed[at : at + size])
+        at += size
+    return (
+        layer_out,
+        input_grad,
+        in_grad,
+        parts[0],
+        parts[1],
+        out_grad,
+        parts[2],
+        up_grad,
+        parts[3],
+        down_grad,
+        parts[4],
+        parts[5],
+        parts[6],
+        parts[7],
+        parts[8],
+    )
+
+
 def solution(mesh):
     placed = (
         P("fsdp", "ctx", None),
@@ -345,7 +511,7 @@
         P("fsdp", "ctx", None),
     )
     return jax.shard_map(
-        body,
+        body_heads if mesh.shape["ctx"] == H else body_general,
         mesh=mesh,
         in_specs=placed,
         out_specs=(

time: 1300 us -> 696 us (0.54)
  waiting for transfers between devices: 1030 us -> 455 us
  matrix products: 113 us -> 89.7 us
  starting transfers between devices: 0.4 us -> 16.8 us
  local copies, waits for them, and re-layouts: 41.4 us -> 25.8 us
    reduce_scatter x5 -> x4, waiting for transfers between devices: 906 us -> 403 us  [scattered(): lax.psum_scatter(grad.astype(low), ('ctx', 'fsdp'), scatter_dimension=0,...]
    all_gather x5 -> x4, waiting for transfers between devices: 121 us -> 15.4 us  [the longest x1 15.4 us: body_heads(): in_full = lax.all_gather(in_weight, 'fsdp', axis=0, tiled=True)]
    dot_general x10 -> x6, matrix products: 67.8 us -> 26.8 us  [the longest x1 9.32 us: body_heads(): jnp.dot(normed_two, up_full, preferred_element_type=jnp.float32) + up_shift]
    all_to_all x0 -> x3, waiting for transfers between devices: none -> 34.7 us  [the longest x2 25.8 us: to_heads(): out = lax.all_to_all(parts, 'ctx', split_axis=2, concat_axis=0, tiled=True)]
    all_to_all x0 -> x1, blocking collectives: none -> 25.5 us  [to_tokens(): out = lax.all_to_all(parts, 'ctx', split_axis=0, concat_axis=2, tiled=True)]
    slice x5 -> x8, local copies, waits for them, and re-layouts: 23.3 us -> 2.2 us  [the longest x2 1.2 us: body_heads(): parts.append(summed[at:at + size])]
    all_to_all x0 -> x3, starting transfers between devices: none -> 15.6 us  [the longest x2 10.3 us: to_heads(): out = lax.all_to_all(parts, 'ctx', split_axis=2, concat_axis=0, tiled=True)]
    all_gather x9 -> x1, blocking collectives: 16.4 us -> 1.95 us  [body_heads(): packed = lax.all_gather(packed, 'fsdp', axis=0).astype(jnp.float32)]
  transfers between devices with their start and end apart: 10 -> 11, of which waited for: 8 -> 7; matrix products, arithmetic and copies ran while one was open for 10% -> 17% of each run, Pallas kernels for 0% -> 0%
where the time goes in v1:
time: 696 us; the launch traced here: 692 us
  waiting for transfers between devices  455 us (65%)
  matrix products  89.7 us (13%)
  blocking collectives  66.7 us (10%)
  local copies, waits for them, and re-layouts  25.8 us (4%)
  other arithmetic  22.4 us (3%)
  starting transfers between devices  16.8 us (2%)
  between operations  15.2 us (2%)
    reduce_scatter x4, waiting for transfers between devices, scattered(): lax.psum_scatter(grad.astype(low), ('ctx', 'fsdp'), scatter_dimension=0,...  403 us
    unnamed x1, blocking collectives  39.2 us
    dot_general x7, matrix products, times_transposed(): jnp.einsum('tg,fg->tf', left, right, preferred_element_type=jnp.float32)  33.4 us
    dot_general x6, matrix products, inner_rows(): jnp.einsum('tf,tg->fg', left, right, preferred_element_type=jnp.float32)  29.5 us
    all_to_all x2, waiting for transfers between devices, to_heads(): out = lax.all_to_all(parts, 'ctx', split_axis=2, concat_axis=0, tiled=True)  25.8 us
    all_to_all x1, blocking collectives, to_tokens(): out = lax.all_to_all(parts, 'ctx', split_axis=0, concat_axis=2, tiled=True)  25.5 us
    all_gather x1, waiting for transfers between devices, body_heads(): in_full = lax.all_gather(in_weight, 'fsdp', axis=0, tiled=True)  15.4 us
  transfers between devices with their start and end apart: 11, of which 7 were waited for; matrix products, arithmetic and copies ran while one was open for 17% of the time, Pallas kernels for 0%

profile of v1, /device:TPU:0, one launch (start us, length us, event | category | flops | bytes accessed | tf_op | source)
XLA Modules:
  0.0 691.8 jit_solution(13350818777161685295)
XLA Ops:
  11.4 1.9 all_gather.15
  13.7 15.4 %all-gather.5.cloned.1.call-done = bf16[1024,3072]{1,0:T(8,128)(2,1)} async-done(((bf16[512,3072]{1,0:T(8,128)(2,1)}), bf16[1024,3072]{1,0:T(8,128)(2,1)}) %all-gather.5.cloned.1.call-update) | async-done | bytes 6291472 | tf_op jit(solution)/shard_map/all_gather | solution.py:364
  29.1 3.9 fusion.50
  33.8 0.9 copy.121
  34.7 6.8 all-to-all-start
  42.5 19.1 %all-to-all-done = bf16[128,3,16,64]{0,3,1,2:T(8,128)(2,1)S(1)} async-done(((bf16[128,3,16,64]{0,3,1,2:T(8,128)(2,1)}), bf16[128,3,16,64]{0,3,1,2:T(8,128)(2,1)S(1)}, u32[]{:S(2)}, u32[]{:S(2)}) %all-to-all-start) | async-done | bytes 786464 | tf_op jit(solution)/shard_map/all_to_all | solution.py:388
  62.5 3.5 fusion.81
  66.0 5.2 select_reduce_fusion
  71.7 4.2 fusion.68
  78.3 1.1 reshape.277
  79.4 5.2 all-to-all-start.1
  84.6 8.9 %all-to-all-done.1 = bf16[16,2,4096]{2,1,0:T(2,128)(2,1)S(1)} async-done(((bf16[16,2,4096]{2,1,0:T(2,128)(2,1)}), bf16[16,2,4096]{2,1,0:T(2,128)(2,1)S(1)}, u32[]{:S(2)}, u32[]{:S(2)}) %all-to-all-start.1) | async-done | bytes 262176 | tf_op jit(solution)/shard_map/all_to_all | solution.py:393
  94.9 2.1 fusion.82
  97.3 9.3 %multiply_convert_fusion.1 = (bf16[128,4096]{1,0:T(8,128)(2,1)}, f32[128,4096]{1,0:T(8,128)}) fusion(f32[4096]{0:T(1024)S(1)} %bitcast.220, bf16[1024,4096]{1,0:T(8,128)(2,1)} %all-gather.9.cloned.1.call-done, f32[128,1024]{1,0:T(8,128)S(1)} %get-tuple-element.53, f32[1024]{0:T(1024)S(1)} %bitcast.207, f32[1024]{0:T(1024)S(1)} %bitcast.203, ...), kind=kOutput, calls=%fused_computation.27 | convolution fusion | flops 1109000192 | bytes 12084224 | tf_op jit(solution)/shard_map/dot_general | solution.py:407
  106.6 9.9 %convert_reduce_fusion = (f32[4096]{0:T(1024)S(1)}, bf16[128,4096]{1,0:T(8,128)(2,1)S(1)}) fusion(f32[128,4096]{1,0:T(8,128)} %get-tuple-element.55, bf16[4096,1024]{1,0:T(8,128)(2,1)} %all-gather.11.cloned.1.call-done, bf16[1,128,1024]{2,1,0:T(8,128)(2,1)S(1)} %copy-done.5), kind=kOutput, calls=%fused_computation.25 | convolution fusion | flops 1112535040 | bytes 11812864 | tf_op jit(solution)/shard_map/tg,fg->tf/dot_general | solution.py:51
  116.6 3.0 multiply_reduce_fusion
  120.1 1.1 copy-done.2
  122.9 3.5 all-to-all-start.2
  126.5 2.0 convolution_convert_fusion.5
  128.8 6.7 all-to-all-done.2
  135.8 9.5 %multiply_convert_fusion = bf16[2048,2048]{0,1:T(8,128)(2,1)S(1)} fusion(f32[2048,2048]{0,1:T(8,128)} %copy-done, f32[2048]{0:T(1024)S(1)} %multiply_reduce_fusion.1, f32[2048]{0:T(1024)S(1)} %log_add_fusion, s32[2048]{0:T(1024)S(1)} %bitcast.213, s32[2048]{0:T(1024)S(1)} %broadcast_add_fusion, bf16[2048,3,64]{0,2,1:T(8,128)(2,1)S(1)} %reshape.265, ...), kind=kOutput, calls=%fused_computation | convolution fusion | flops 570425344 | bytes 25739264 | tf_op jit(solution)/shard_map/tg,fg->tf/dot_general | solution.py:51
  145.3 2.7 fusion.4
  147.9 1.6 fusion.6
  149.5 8.0 %fusion.5 = bf16[2048,1,1,64]{0,3,2,1:T(8,128)(2,1)S(1)} fusion(bf16[8,8,16,128]{3,2,1,0:T(8,128)(2,1)S(1)} %bitcast.189, f32[2048,2048]{0,1:T(8,128)} %copy-done, f32[2048]{0:T(1024)S(1)} %log_add_fusion, s32[2048]{0:T(1024)S(1)} %bitcast.214, s32[2048]{0:T(1024)S(1)} %broadcast_add_fusion), kind=kOutput, calls=%fused_computation.20 | convolution fusion | flops 562167808 | bytes 17326080 | tf_op jit(solution)/shard_map/tf,tg->fg/dot_general | solution.py:47
  157.5 1.0 pad_maximum_fusion.2
  158.5 2.8 copy.130
  161.4 2.5 reshape.279
  163.9 25.5 %all_to_all.60 = bf16[16,2,12288]{2,1,0:T(2,128)(2,1)} all-to-all(bf16[16,2,12288]{2,1,0:T(2,128)(2,1)} %reshape.279), channel_id=1, replica_groups=mesh['ctx'=16,'fsdp'=2] {'ctx'}, dimensions={0} | all-to-all | bytes 1572864 | tf_op jit(solution)/shard_map/all_to_all | solution.py:393
  189.4 2.9 reshape.280
  192.3 2.2 copy.137
  194.4 3.1 fusion.48
  198.8 3.3 pad_maximum_fusion
  202.4 6.9 convolution_convert_fusion.1
  209.4 6.9 convolution_convert_fusion
  216.5 5.7 fusion.24
  222.2 1.9 copy.136
  224.1 1.6 convert_reduce_fusion.1
  226.0 3.9 fusion.2
  229.9 2.7 fusion.77
  233.0 1.0 convert_reduce_fusion.3
  234.3 39.2 %all-reduce = f32[32,384]{1,0:T(8,128)S(1)} all-reduce(f32[32,384]{1,0:T(8,128)S(1)} %concatenate.39), channel_id=3, replica_groups=mesh['ctx'=16,'fsdp'=2] {'ctx','fsdp'}, use_global_device_ids=true, to_apply=%region_22.23.clone | all-reduce | flops 12288 | bytes 98304
  274.8 1.5 convert_element_type.123
  276.3 109.0 %reduce-scatter.5.cloned.1.call-done = bf16[32,3072]{1,0:T(8,128)(2,1)} async-done(((bf16[1024,3072]{1,0:T(8,128)(2,1)}), bf16[32,3072]{1,0:T(8,128)(2,1)}) %reduce-scatter.5.cloned.1.call-update) | async-done | bytes 196624 | tf_op jit(solution)/shard_map/reduce_scatter | solution.py:416
  385.3 1.7 convert_element_type.118
  387.0 148.7 %reduce-scatter.9.cloned.1.call-done = bf16[32,4096]{1,0:T(8,128)(2,1)} async-done(((bf16[1024,4096]{1,0:T(8,128)(2,1)}), bf16[32,4096]{1,0:T(8,128)(2,1)}) %reduce-scatter.9.cloned.1.call-update) | async-done | bytes 262160 | tf_op jit(solution)/shard_map/reduce_scatter | solution.py:416
  535.8 1.8 convert_element_type.125
  537.5 145.2 %reduce-scatter.11.cloned.1.call-done = bf16[128,1024]{1,0:T(8,128)(2,1)} async-done(((bf16[4096,1024]{1,0:T(8,128)(2,1)}), bf16[128,1024]{1,0:T(8,128)(2,1)}) %reduce-scatter.11.cloned.1.call-update) | async-done | bytes 262160 | tf_op jit(solution)/shard_map/reduce_scatter | solution.py:416
  682.7 1.8 convert_element_type.127
  (131 shorter events, 18.1 us)
Async XLA Ops:
  7.2 21.9 %all-gather.5.cloned.1.call-start = ((), (), s32[]{:S(2)}) async-start(), calls=%async_computation.8 | async-start | bytes 9437184 | tf_op jit(solution)/shard_map/all_gather | solution.py:364
  7.9 87.0 %all-gather.7.cloned.1.call-start = ((), (), s32[]{:S(2)}) async-start(), calls=%async_computation.9 | async-start | bytes 3145728 | tf_op jit(solution)/shard_map/all_gather | solution.py:365
  8.7 0.8 copy-start.11
  8.7 1.1 copy-start.12
  8.7 1.3 copy-start.13
  8.7 1.5 copy-start.14
  8.7 1.7 copy-start.15
  8.7 1.9 copy-start.16
  8.7 2.2 copy-start.17
  8.7 2.4 copy-start.18
  8.7 2.6 copy-start.10
  8.8 4.6 copy-start.1
  8.8 88.5 %all-gather.9.cloned.1.call-start = ((), (), s32[]{:S(2)}) async-start(), calls=%async_computation.10 | async-start | bytes 12582912 | tf_op jit(solution)/shard_map/all_gather | solution.py:366
  34.7 26.9 %all-to-all-start = ((bf16[128,3,16,64]{0,3,1,2:T(8,128)(2,1)}), bf16[128,3,16,64]{0,3,1,2:T(8,128)(2,1)S(1)}, u32[]{:S(2)}, u32[]{:S(2)}) async-start(bf16[128,3,16,64]{0,3,1,2:T(8,128)(2,1)} %copy.121), calls=%async_computation | async-start | bytes 1572864 | tf_op jit(solution)/shard_map/all_to_all | solution.py:388
  41.5 0.7 copy-start.19
  41.5 0.8 copy-start.9
  41.5 65.1 %all-gather.11.cloned.1.call-start = ((), (), s32[]{:S(2)}) async-start(), calls=%async_computation.11 | async-start | bytes 12582912 | tf_op jit(solution)/shard_map/all_gather | solution.py:367
  66.0 5.7 copy-start
  75.9 0.8 copy-start.7
  79.4 14.1 %all-to-all-start.1 = ((bf16[16,2,4096]{2,1,0:T(2,128)(2,1)}), bf16[16,2,4096]{2,1,0:T(2,128)(2,1)S(1)}, u32[]{:S(2)}, u32[]{:S(2)}) async-start(bf16[16,2,4096]{2,1,0:T(2,128)(2,1)} %reshape.277), calls=%async_computation.1 | async-start | bytes 524288 | tf_op jit(solution)/shard_map/all_to_all | solution.py:393
  97.3 9.3 %copy-start.5 = (bf16[1,128,1024]{2,1,0:T(8,128)(2,1)S(1)}, bf16[1,128,1024]{2,1,0:T(8,128)(2,1)}, u32[]{:S(2)}) copy-start(bf16[1,128,1024]{2,1,0:T(8,128)(2,1)} %param.33) | copy-start | bytes 786436
  106.6 9.9 %copy-start.3 = (bf16[1024,4096]{1,0:T(8,128)(2,1)S(1)}, bf16[1024,4096]{1,0:T(8,128)(2,1)}, u32[]{:S(2)}) copy-start(bf16[1024,4096]{1,0:T(8,128)(2,1)} %all-gather.9.cloned.1.call-done) | copy-start | bytes 25165828
  116.6 3.1 copy-start.4
  119.6 1.6 copy-start.2
  122.9 12.6 %all-to-all-start.2 = ((bf16[128,1,16,64]{0,3,1,2:T(8,128)(2,1)}), bf16[128,1,16,64]{0,3,1,2:T(8,128)(2,1)S(1)}, u32[]{:S(2)}, u32[]{:S(2)}) async-start(bf16[128,1,16,64]{0,3,1,2:T(8,128)(2,1)} %bitcast.27), calls=%async_computation.2 | async-start | bytes 524288 | tf_op jit(solution)/shard_map/all_to_all | solution.py:388
  126.5 9.2 %copy-start.8 = (f32[2048,64]{0,1:T(8,128)S(1)}, f32[2048,64]{0,1:T(8,128)}, u32[]{:S(2)}) copy-start(f32[2048,64]{0,1:T(8,128)} %copy-done.7) | copy-start | bytes 1572868
  126.5 148.3 %reduce-scatter.7.cloned.1.call-start = ((), (), s32[]{:S(2)}) async-start(), calls=%async_computation.13 | async-start | bytes 2162688 | tf_op jit(solution)/shard_map/reduce_scatter | solution.py:416
  128.6 256.8 %reduce-scatter.5.cloned.1.call-start = ((), (), s32[]{:S(2)}) async-start(), calls=%async_computation.12 | async-start | bytes 6488064 | tf_op jit(solution)/shard_map/reduce_scatter | solution.py:416
  202.1 333.6 %reduce-scatter.9.cloned.1.call-start = ((), (), s32[]{:S(2)}) async-start(), calls=%async_computation.14 | async-start | bytes 8650752 | tf_op jit(solution)/shard_map/reduce_scatter | solution.py:416
  209.4 473.3 %reduce-scatter.11.cloned.1.call-start = ((), (), s32[]{:S(2)}) async-start(), calls=%async_computation.15 | async-start | bytes 8650752 | tf_op jit(solution)/shard_map/reduce_scatter | solution.py:416
  229.9 3.1 copy-start.6
Sparse Core Ops, SparseCore 0:
  9.6 19.5 all-gather.4
  30.7 11.7 all-gather.6
  44.0 21.0 all-gather.8
  66.5 21.0 all-gather.10
  129.3 139.2 reduce-scatter.6
  275.0 110.2 reduce-scatter.4
  387.6 148.0 reduce-scatter.8
  538.0 144.6 reduce-scatter.10

commit v2 on v0

--- a/solution.py
+++ b/solution.py
@@ -1,6 +1,9 @@
 import jax
 import jax.numpy as jnp
 from jax import lax
+from typing import Any, NamedTuple
+from jax.experimental import pallas as pl
+from jax.experimental.pallas import tpu as pltpu
 from jax.sharding import PartitionSpec as P
 
 H = 16
@@ -63,7 +66,7 @@
     )
 
 
-def body(
+def body_general(
     tokens,
     in_weight,
     query_bias,
@@ -324,6 +327,877 @@
     )
 
 
+MESH_ID = pl.DeviceIdType.MESH
+LOW = jnp.bfloat16
+F32 = jnp.float32
+T = 128
+
+
+def dot(left, right):
+    return jnp.dot(left, right, preferred_element_type=jnp.float32)
+
+
+def dot_nt(left, right):
+    return lax.dot_general(left, right, (((1,), (1,)), ((), ())), preferred_element_type=F32)
+
+
+def dot_tn(left, right):
+    return lax.dot_general(left, right, (((0,), (0,)), ((), ())), preferred_element_type=F32)
+
+
+def turned(block):
+    return block.astype(F32).T
+
+
+def standard(values):
+    center = values - jnp.mean(values, axis=1, keepdims=True)
+    spread = lax.rsqrt(jnp.mean(center * center, axis=1, keepdims=True) + epsilon)
+    return center * spread, spread
+
+
+def standard_back(grad, gain, unit, spread):
+    e = grad * gain
+    return spread * (
+        e - jnp.mean(e, axis=1, keepdims=True) - unit * jnp.mean(e * unit, axis=1, keepdims=True)
+    )
+
+
+def gelu_pair(hidden):
+    phi = 0.5 * (1.0 + lax.erf(hidden * 0.7071067811865476))
+    density = jnp.exp(hidden * hidden * -0.5) * 0.3989422804014327
+    return hidden * phi, phi + hidden * density
+
+
+def lanes(index, size):
+    return pl.ds(pl.multiple_of(index * size, size), size)
+
+
+def column_sum(values):
+    return jnp.sum(values, axis=0, keepdims=True)
+
+
+class Sems(NamedTuple):
+    send: Any
+    recv: Any
+
+
+class Scratch(NamedTuple):
+    vec: Any
+    bias: Any
+    in_full: Any
+    out_full: Any
+    up_full: Any
+    down_full: Any
+    normed_one: Any
+    send_qkv: Any
+    qkv_t: Any
+    kv: Any
+    scores: Any
+    lse: Any
+    delta: Any
+    head_out: Any
+    send_head: Any
+    att_t: Any
+    att_all: Any
+    att: Any
+    middle: Any
+    grad_middle: Any
+    cot_all: Any
+    two_all: Any
+    branch_all: Any
+    acc_out: Any
+    acc_grad: Any
+    grad_hidden: Any
+    vec_grad: Any
+    do_t: Any
+    q_rows: Any
+    do_rows: Any
+    dkv: Any
+    down_mine: Any
+    down_theirs: Any
+    down_pair: Any
+    down_line: Any
+    up_mine: Any
+    up_theirs: Any
+    up_pair: Any
+    up_line: Any
+    up_piece: Any
+    out_mine: Any
+    out_theirs: Any
+    out_pair: Any
+    out_line: Any
+    dqkv: Any
+    gp_t: Any
+    in_mine: Any
+    in_theirs: Any
+    in_pair: Any
+    in_send: Any
+    in_recv: Any
+    vec_send: Any
+    vec_recv: Any
+    vec_mine: Any
+    vec_pair: Any
+    sem_load: Any
+    sem_pair: Any
+    sem_qkv: Any
+    sem_one: Any
+    sem_relay: Any
+    sem_cot: Any
+    sem_head: Any
+    sem_att: Any
+    sem_two: Any
+    sem_back: Any
+    sem_branch: Any
+    sem_line: Any
+    sem_grads: Any
+    sem_up: Any
+    sem_in: Any
+    sem_vec: Any
+    sem_one_load: Any
+
+
+def scratch():
+    def v(shape, kind):
+        return pltpu.VMEM(shape, kind)
+
+    def sems(count):
+        return Sems(pltpu.SemaphoreType.DMA((count,)), pltpu.SemaphoreType.DMA((count,)))
+
+    return Scratch(
+        vec=v((2, 12, 1, 512), F32),
+        bias=v((2, 1, 1024), F32),
+        in_full=v((1024, 3072), LOW),
+        out_full=v((1024, 1024), LOW),
+        up_full=v((1024, 4096), LOW),
+        down_full=v((4096, 1024), LOW),
+        normed_one=v((128, 1024), LOW),
+        send_qkv=v((16, 192, 128), LOW),
+        qkv_t=v((192, 2048), LOW),
+        kv=v((2048, 128), LOW),
+        scores=v((2048, 256), F32),
+        lse=v((1, 2048), F32),
+        delta=v((1, 2048), F32),
+        head_out=v((64, 2048), F32),
+        send_head=v((16, 64, 128), LOW),
+        att_t=v((16, 64, 128), LOW),
+        att_all=v((4, 4, 64, 128), LOW),
+        att=v((128, 1024), LOW),
+        middle=v((128, 1024), F32),
+        grad_middle=v((128, 1024), F32),
+        cot_all=v((4, 128, 1024), LOW),
+        two_all=v((4, 128, 1024), LOW),
+        branch_all=v((4, 128, 1024), LOW),
+        acc_out=v((128, 1024), F32),
+        acc_grad=v((128, 1024), F32),
+        grad_hidden=v((512, 1024), LOW),
+        vec_grad=v((16, 1024), F32),
+        do_t=v((64, 2048), LOW),
+        q_rows=v((2048, 128), LOW),
+        do_rows=v((2048, 128), LOW),
+        dkv=v((2048, 128), F32),
+        down_mine=v((4, 128, 1024), F32),
+        down_theirs=v((4, 128, 1024), LOW),
+        down_pair=v((4, 128, 1024), LOW),
+        down_line=v((3, 128, 1024), LOW),
+        up_mine=v((4, 128, 1024), F32),
+        up_theirs=v((4, 128, 1024), LOW),
+        up_pair=v((4, 128, 1024), LOW),
+        up_line=v((3, 128, 1024), LOW),
+        up_piece=v((4, 32, 1024), F32),
+        out_mine=v((4, 32, 1024), F32),
+        out_theirs=v((4, 32, 1024), LOW),
+        out_pair=v((4, 32, 1024), LOW),
+        out_line=v((3, 32, 1024), LOW),
+        dqkv=v((16, 192, 128), LOW),
+        gp_t=v((3072, 128), LOW),
+        in_mine=v((16, 32, 256), F32),
+        in_theirs=v((16, 32, 256), LOW),
+        in_pair=v((16, 32, 256), LOW),
+        in_send=v((16, 32, 256), LOW),
+        in_recv=v((16, 32, 256), LOW),
+        vec_send=v((8, 16, 128), F32),
+        vec_recv=v((16, 16, 128), F32),
+        vec_mine=v((16, 128), F32),
+        vec_pair=v((16, 128), F32),
+        sem_load=sems(6),
+        sem_pair=sems(10),
+        sem_qkv=sems(16),
+        sem_one=sems(16),
+        sem_relay=sems(12),
+        sem_cot=sems(3),
+        sem_head=sems(16),
+        sem_att=sems(3),
+        sem_two=sems(3),
+        sem_back=sems(16),
+        sem_branch=sems(3),
+        sem_line=sems(9),
+        sem_grads=sems(16),
+        sem_up=sems(12),
+        sem_in=sems(16),
+        sem_vec=sems(16),
+        sem_one_load=pltpu.SemaphoreType.DMA((16,)),
+    )
+
+
+def layer_kernel(
+    tok_ref,
+    cot_ref,
+    vec_ref,
+    key_ref,
+    query_ref,
+    in_hbm,
+    out_hbm,
+    up_hbm,
+    down_hbm,
+    layer_out,
+    input_grad,
+    in_out,
+    out_out,
+    up_out,
+    down_out,
+    vec_out,
+    one_hbm,
+    s,
+):
+    n = 16
+    scale = HD ** (-0.5)
+    c, f = lax.axis_index("ctx"), lax.axis_index("fsdp")
+    z, p = c // 4, c % 4
+    y, x = p // 2, p % 2
+    home = c - p
+    sibling = (c, 1 - f)
+    plane_places = [2 * y + 1 - x, 2 * (1 - y) + x, 2 * (1 - y) + 1 - x]
+    planes = [(home + place, f) for place in plane_places]
+    z_peers = [((z + k) % 4) for k in range(1, 4)]
+    first_core = f == 0
+
+    def remote(src, dst, sems, i, j, device):
+        return pltpu.make_async_remote_copy(
+            src_ref=src,
+            dst_ref=dst,
+            send_sem=sems.send.at[i],
+            recv_sem=sems.recv.at[j],
+            device_id=device,
+            device_id_type=MESH_ID,
+        )
+
+    def each_peer(step):
+        def one(k, carry):
+            step((c + k) % n)
+            return carry
+
+        lax.fori_loop(1, n, one, 0)
+
+    def to_planes(src_of, dst, sems):
+        copies = []
+        for i in range(3):
+            copy = remote(src_of(i), dst.at[1 + i], sems, i, i, planes[i])
+            copy.start()
+            copies.append(copy)
+        return copies
+
+    barrier = pltpu.get_barrier_semaphore()
+
+    def greet(peer):
+        pl.semaphore_signal(barrier, inc=1, device_id=(peer, f), device_id_type=MESH_ID)
+
+    each_peer(greet)
+    pl.semaphore_signal(barrier, inc=1, device_id=sibling, device_id_type=MESH_ID)
+    weights = [
+        (in_hbm, s.in_full, 512),
+        (out_hbm, s.out_full, 512),
+        (up_hbm, s.up_full, 512),
+        (down_hbm, s.down_full, 2048),
+    ]
+    loads, pairs = [], []
+    for i, (src, dst, size) in enumerate(weights):
+        load = pltpu.make_async_copy(src, dst.at[pl.ds(f * size, size)], s.sem_load.send.at[i])
+        load.start()
+        loads.append(load)
+    s.vec[f] = vec_ref[...]
+    pl.semaphore_wait(barrier, n)
+    vec_copy = remote(vec_ref, s.vec.at[f], s.sem_pair, 4, 4, sibling)
+    vec_copy.start()
+    for i, (src, dst, size) in enumerate(weights):
+        pair = remote(src, dst.at[pl.ds(f * size, size)], s.sem_pair, i, i, sibling)
+        pair.start()
+        pairs.append(pair)
+    sent = [vec_copy] + pairs
+
+    def row(i):
+        return jnp.concatenate([s.vec[0, i], s.vec[1, i]], axis=1)
+
+    unit_one, unused = standard(tok_ref[...].astype(F32))
+    vec_copy.wait_recv()
+    s.normed_one[...] = (unit_one * row(4) + row(5)).astype(LOW)
+    s.bias[0] = row(0)
+    s.bias[1] = row(1)
+    loads[0].wait()
+    pairs[0].wait_recv()
+
+    def qkv_copy(dst):
+        return remote(
+            s.send_qkv.at[dst], s.qkv_t.at[:, lanes(c, T)], s.sem_qkv, dst, c, (dst, f)
+        )
+
+    def project(g, carry):
+        group = (z + g) % 4
+        for part in range(3):
+            at = pl.ds(pl.multiple_of(part * 1024 + group * 256, 256), 256)
+            acc = dot(s.normed_one[...], s.in_full[:, at])
+            if part == 0:
+                acc = (acc + s.bias[0, :, lanes(group, 256)]) * scale
+            if part == 2:
+                acc = acc + s.bias[1, :, lanes(group, 256)]
+            for u in range(2):
+                block = acc[:, u * T : (u + 1) * T].T.astype(LOW)
+                for w in range(2):
+                    s.send_qkv[group * 4 + 2 * u + w, part * 64 : part * 64 + 64, :] = block[
+                        w * 64 : w * 64 + 64
+                    ]
+        for u in range(4):
+            dst = group * 4 + u
+
+            @pl.when(dst != c)
+            def _():
+                qkv_copy(dst).start()
+
+            @pl.when(dst == c)
+            def _():
+                s.qkv_t[:, lanes(c, T)] = s.send_qkv[dst]
+
+        return carry
+
+    lax.fori_loop(0, 4, project, 0)
+    keep = pltpu.make_async_copy(s.normed_one, one_hbm.at[c], s.sem_load.send.at[4])
+    keep.start()
+    for k in range(3):
+        copy = remote(s.normed_one, one_hbm.at[c], s.sem_one, k, c, (z_peers[k] * 4 + p, f))
+        copy.start()
+        sent.append(copy)
+    s.cot_all[0] = cot_ref[...]
+    cot_copies = to_planes(lambda i: cot_ref, s.cot_all, s.sem_cot)
+    sent += cot_copies
+
+    def qkv_arrived(src):
+        remote(
+            s.send_qkv.at[src], s.qkv_t.at[:, lanes(src, T)], s.sem_qkv, src, src, (src, f)
+        ).wait_recv()
+
+    each_peer(qkv_arrived)
+
+    for i in range(n):
+        at = slice(i * T, i * T + T)
+        s.kv[at] = turned(s.qkv_t[64:192, at]).astype(LOW)
+    nothing = jnp.zeros((64, 256), LOW)
+
+    def seen(keys, at):
+        place = jnp.concatenate([key_ref[keys], key_ref[keys]], axis=1)
+        return (place >= query_ref[1:2, at]) & (place <= query_ref[0:1, at])
+
+    def head_copy(dst):
+        return remote(s.send_head.at[dst], s.att_t.at[p * 4 + z], s.sem_head, dst, c, (dst, f))
+
+    def forward(i, carry):
+        block = (c // 2 + i) % 8
+        at = lanes(block, 256)
+        query = jnp.concatenate([s.qkv_t[0:64, at], nothing], axis=0)
+        top = jnp.full((8, 256), far_below, F32)
+        for k in range(8):
+            keys = slice(k * 256, k * 256 + 256)
+            score = jnp.where(seen(keys, at), dot(s.kv[keys], query), far_below)
+            s.scores[keys] = score
+            top = jnp.maximum(top, jnp.max(score.reshape(32, 8, 256), axis=0))
+        top = jnp.max(top, axis=0, keepdims=True)
+        total = jnp.zeros((8, 256), F32)
+        acc = jnp.zeros((64, 256), F32)
+        for k in range(8):
+            keys = slice(k * 256, k * 256 + 256)
+            grown = jnp.exp(s.scores[keys] - top)
+            total = total + jnp.sum(grown.reshape(32, 8, 256), axis=0)
+            acc = acc + dot(s.qkv_t[128:192, keys], grown.astype(LOW))
+        total = column_sum(total)
+        s.lse[:, at] = top + jnp.log(total)
+        result = acc / total
+        s.head_out[:, at] = result
+        for u in range(2):
+            dst = block * 2 + u
+            s.send_head[dst] = result[:, u * T : u * T + T].astype(LOW)
+
+            @pl.when(dst != c)
+            def _():
+                head_copy(dst).start()
+
+            @pl.when(dst == c)
+            def _():
+                s.att_t[p * 4 + z] = s.send_head[dst]
+
+        return carry
+
+    lax.fori_loop(0, 8, forward, 0)
+
+    def head_arrived(src):
+        slot = (src % 4) * 4 + src // 4
+        remote(s.send_head.at[src], s.att_t.at[slot], s.sem_head, src, src, (src, f)).wait_recv()
+
+    each_peer(head_arrived)
+    s.att_all[0] = s.att_t[pl.ds(p * 4, 4)]
+    att_copies = to_planes(
+        lambda i: s.att_t.at[pl.ds(plane_places[i] * 4, 4)], s.att_all, s.sem_att
+    )
+    sent += att_copies
+    for i in range(8):
+        slots = [(h % 4) * 4 + h // 4 for h in (2 * i, 2 * i + 1)]
+        block = jnp.concatenate([s.att_t[slots[0]], s.att_t[slots[1]]], axis=0)
+        s.att[:, i * T : i * T + T] = turned(block).astype(LOW)
+
+    loads[1].wait()
+    pairs[1].wait_recv()
+    middle = tok_ref[...].astype(F32) + dot(s.att[...], s.out_full[...]) + row(2)
+    s.middle[...] = middle
+    unit_two, unused = standard(middle)
+    s.two_all[0] = (unit_two * row(6) + row(7)).astype(LOW)
+    two_copies = to_planes(lambda i: s.two_all.at[0], s.two_all, s.sem_two)
+    sent += two_copies
+    for i in (2, 3):
+        loads[i].wait()
+        pairs[i].wait_recv()
+    s.acc_out[...] = jnp.zeros((T, 1024), F32)
+    s.acc_grad[...] = jnp.zeros((T, 1024), F32)
+    s.vec_grad[...] = jnp.zeros((16, 1024), F32)
+
+    def feed(j, carry):
+        at = lanes(j, 512)
+        hidden = dot(s.two_all[0], s.up_full[:, at]) + s.vec[j // 4, 8 + j % 4]
+        active, slope = gelu_pair(hidden)
+        grad_active = dot_nt(cot_ref[...], s.down_full[at, :])
+        grad_hidden = (grad_active * slope).astype(LOW)
+        s.acc_out[...] += dot(active.astype(LOW), s.down_full[at, :])
+        s.acc_grad[...] += dot_nt(grad_hidden, s.up_full[:, at])
+        summed = column_sum(grad_hidden.astype(F32))
+        for q in range(4):
+            s.vec_grad[8 + q : 9 + q, lanes(j, T)] = summed[:, q * T : q * T + T]
+        return carry
+
+    lax.fori_loop(0, 8, feed, 0)
+    layer_out[...] = (s.middle[...] + s.acc_out[...] + row(3)).astype(LOW)
+    grad_result = cot_ref[...].astype(F32)
+    s.vec_grad[3:4] = column_sum(grad_result)
+    unit_two, spread_two = standard(s.middle[...])
+    grad_two = s.acc_grad[...]
+    s.vec_grad[6:7] = column_sum(grad_two * unit_two)
+    s.vec_grad[7:8] = column_sum(grad_two)
+    grad_middle = grad_result + standard_back(grad_two, row(6), unit_two, spread_two)
+    s.grad_middle[...] = grad_middle
+    branch = grad_middle.astype(LOW)
+    s.branch_all[0] = branch
+    s.vec_grad[2:3] = column_sum(branch.astype(F32))
+
+    def head_done(dst):
+        head_copy(dst).wait_send()
+
+    each_peer(head_done)
+    for i in range(4):
+        at = slice(i * 256, i * 256 + 256)
+        part = dot_nt(s.out_full[at, :], branch).astype(LOW)
+        s.send_head[4 * i : 4 * i + 4] = part.reshape(4, 64, T)
+
+    def back_copy(dst):
+        return remote(s.send_head.at[dst], s.do_t.at[:, lanes(c, T)], s.sem_back, dst, c, (dst, f))
+
+    each_peer(lambda dst: back_copy(dst).start())
+    s.do_t[:, lanes(c, T)] = s.send_head[c]
+    branch_copies = to_planes(lambda i: s.branch_all.at[0], s.branch_all, s.sem_branch)
+    sent += branch_copies
+
+    def one_arrived(src):
+        remote(s.normed_one, one_hbm.at[src], s.sem_one, 0, src, (src, f)).wait_recv()
+
+    keep.wait()
+    for k in range(3):
+        one_arrived(z_peers[k] * 4 + p)
+    for k in range(4):
+        slot = (c if k == 0 else z_peers[k - 1] * 4 + p)
+        for i in range(3):
+            copy = pltpu.make_async_remote_copy(
+                src_ref=one_hbm.at[slot],
+                dst_ref=one_hbm.at[slot],
+                send_sem=s.sem_relay.send.at[k * 3 + i],
+                recv_sem=s.sem_one.recv.at[slot],
+                device_id=planes[i],
+                device_id_type=MESH_ID,
+            )
+            copy.start()
+            sent.append(copy)
+
+    for i in range(3):
+        cot_copies[i].wait_recv()
+        two_copies[i].wait_recv()
+
+    def plane_rows(ref):
+        return ref[...].reshape(512, 1024)
+
+    def strip(q, carry):
+        at = pl.ds(pl.multiple_of(q * 1024 + p * 256, 256), 256)
+        shift = s.vec[q // 2, 8 + (q % 2) * 2 + p // 2, :, lanes(p % 2, 256)]
+        hidden = dot(plane_rows(s.two_all), s.up_full[:, at]) + shift
+        active, slope = gelu_pair(hidden)
+        grad_active = dot_nt(plane_rows(s.cot_all), s.down_full[at, :])
+        s.grad_hidden[:, lanes(q, 256)] = (grad_active * slope).astype(LOW)
+        part = dot_tn(active.astype(LOW), plane_rows(s.cot_all))
+        s.down_mine[q] = jnp.where(first_core, part[:T], part[T:])
+        s.down_theirs[q] = jnp.where(first_core, part[T:], part[:T]).astype(LOW)
+        return carry
+
+    lax.fori_loop(0, 4, strip, 0)
+    down_pair = remote(s.down_theirs, s.down_pair, s.sem_pair, 5, 5, sibling)
+    down_pair.start()
+
+    def split_rows(part):
+        parts = part.reshape(4, 2, 32, 1024)
+        mine = jnp.where(first_core, parts[:, 0], parts[:, 1])
+        theirs = jnp.where(first_core, parts[:, 1], parts[:, 0])
+        return mine, theirs.astype(LOW)
+
+    def up_rows(q, carry):
+        left = s.two_all[:, :, lanes(q, 256)].reshape(512, 256)
+        mine, theirs = split_rows(dot_tn(left, s.grad_hidden[...]))
+        s.up_mine[q] = mine.reshape(T, 1024)
+        s.up_theirs[q] = theirs.reshape(T, 1024)
+        return carry
+
+    lax.fori_loop(0, 4, up_rows, 0)
+    up_pair = remote(s.up_theirs, s.up_pair, s.sem_pair, 6, 6, sibling)
+    up_pair.start()
+
+    def to_line(mine, theirs, pair, line, base):
+        copies = []
+        for k in range(3):
+            at = z_peers[k]
+            theirs[at] = (
+                mine[at] + pair[at].astype(F32)
+            ).astype(LOW)
+            copy = remote(
+                theirs.at[at],
+                line.at[k],
+                s.sem_line,
+                base + k,
+                base + k,
+                (at * 4 + p, f),
+            )
+            copy.start()
+            copies.append(copy)
+        mine[z] += pair[z].astype(F32)
+        return copies
+
+    down_pair.wait()
+    down_line = to_line(s.down_mine, s.down_theirs, s.down_pair, s.down_line, 0)
+    for i in range(3):
+        att_copies[i].wait_recv()
+        branch_copies[i].wait_recv()
+    part = jnp.zeros((256, 1024), F32)
+    for i in range(4):
+        part = part + dot(s.att_all[i].reshape(256, T), s.branch_all[i])
+    mine, theirs = split_rows(part)
+    s.out_mine[...] = mine
+    s.out_theirs[...] = theirs
+    out_pair = remote(s.out_theirs, s.out_pair, s.sem_pair, 7, 7, sibling)
+    out_pair.start()
+    up_pair.wait()
+    up_line = to_line(s.up_mine, s.up_theirs, s.up_pair, s.up_line, 3)
+    out_pair.wait()
+    out_line = to_line(s.out_mine, s.out_theirs, s.out_pair, s.out_line, 6)
+    sent += down_line + up_line + out_line
+
+    def qkv_done(dst):
+        qkv_copy(dst).wait_send()
+
+    each_peer(qkv_done)
+
+    def back_arrived(src):
+        remote(
+            s.send_head.at[src], s.do_t.at[:, lanes(src, T)], s.sem_back, src, src, (src, f)
+        ).wait_recv()
+
+    each_peer(back_arrived)
+    small_nothing = jnp.zeros((64, T), LOW)
+    for i in range(n):
+        at = slice(i * T, i * T + T)
+        s.q_rows[at] = turned(
+            jnp.concatenate([s.qkv_t[0:64, at], small_nothing], axis=0)
+        ).astype(LOW)
+        s.do_rows[at] = turned(
+            jnp.concatenate([small_nothing, s.do_t[:, at]], axis=0)
+        ).astype(LOW)
+    s.delta[...] = column_sum(s.do_t[...].astype(F32) * s.head_out[...])
+    s.dkv[...] = jnp.zeros((2048, 128), F32)
+
+    def backward(block, carry):
+        at = lanes(block, 256)
+        query = jnp.concatenate([s.qkv_t[0:64, at], nothing], axis=0)
+        grad = jnp.concatenate([nothing, s.do_t[:, at]], axis=0)
+        lse, delta = s.lse[:, at], s.delta[:, at]
+        dq = jnp.zeros((64, 256), F32)
+        for k in range(8):
+            keys = slice(k * 256, k * 256 + 256)
+            score = dot(s.kv[keys], query)
+            prob = jnp.where(seen(keys, at), jnp.exp(score - lse), 0.0)
+            grad_prob = dot(s.kv[keys], grad)
+            grad_score = (prob * (grad_prob - delta)).astype(LOW)
+            s.dkv[keys] += dot(grad_score, s.q_rows[at]) + dot(
+                prob.astype(LOW), s.do_rows[at]
+            )
+            dq = dq + dot(s.qkv_t[64:128, keys], grad_score)
+        for u in range(2):
+            s.send_qkv[block * 2 + u, 0:64] = dq[:, u * T : u * T + T].astype(LOW)
+        return carry
+
+    lax.fori_loop(0, 8, backward, 0)
+
+    def grads_copy(dst):
+        return remote(s.send_qkv.at[dst], s.dqkv.at[c], s.sem_grads, dst, c, (dst, f))
+
+    for i in range(n):
+        s.send_qkv[i, 64:192] = s.dkv[i * T : i * T + T].T.astype(LOW)
+    each_peer(lambda dst: grads_copy(dst).start())
+    s.dqkv[c] = s.send_qkv[c]
+
+    for k in range(4):
+        base = (z + k) % 4 * 4
+        for i in range(3):
+            one_arrived(base + plane_places[i])
+    one_full = s.down_full.at[pl.ds(0, 2048)]
+    one_loads = []
+    for i in range(n):
+        load = pltpu.make_async_copy(
+            one_hbm.at[i], s.down_full.at[pl.ds(i * T, T)], s.sem_one_load.at[i]
+        )
+        load.start()
+        one_loads.append(load)
+    for load in one_loads:
+        load.wait()
+    head_grad = jnp.concatenate([s.send_qkv[i] for i in range(n)], axis=1)
+    for i in range(4):
+        part = dot(head_grad, s.down_full[0:2048, i * 256 : i * 256 + 256])
+        part = jnp.concatenate(
+            [part[0:64] * scale, part[64:192], jnp.zeros((64, 256), F32)], axis=0
+        )
+        for u in range(2):
+            parts = part[:, u * T : u * T + T].T.reshape(2, 2, 32, 256)
+            at = slice(4 * i + 2 * u, 4 * i + 2 * u + 2)
+            s.in_mine[at] = jnp.where(first_core, parts[:, 0], parts[:, 1])
+            s.in_theirs[at] = jnp.where(first_core, parts[:, 1], parts[:, 0]).astype(LOW)
+    in_pair = remote(s.in_theirs, s.in_pair, s.sem_pair, 8, 8, sibling)
+    in_pair.start()
+
+    def grads_arrived(src):
+        remote(s.send_qkv.at[src], s.dqkv.at[src], s.sem_grads, src, src, (src, f)).wait_recv()
+
+    in_pair.wait()
+    s.in_send[...] = (s.in_mine[...] + s.in_pair[...].astype(F32)).astype(LOW)
+
+    def in_copy(dst):
+        return remote(s.in_send.at[dst], s.in_recv.at[c], s.sem_in, dst, c, (dst, f))
+
+    each_peer(lambda dst: in_copy(dst).start())
+    s.in_recv[c] = s.in_send[c]
+    each_peer(grads_arrived)
+    for h in range(n):
+        s.gp_t[h * 64 : h * 64 + 64] = s.dqkv[h, 0:64] * jnp.asarray(scale, LOW)
+        s.gp_t[1024 + h * 64 : 1088 + h * 64] = s.dqkv[h, 64:128]
+        s.gp_t[2048 + h * 64 : 2112 + h * 64] = s.dqkv[h, 128:192]
+    ones = jnp.ones((8, T), LOW)
+    s.vec_grad[0:1] = dot_nt(ones, s.gp_t[0:1024])[0:1]
+    s.vec_grad[1:2] = dot_nt(ones, s.gp_t[2048:3072])[0:1]
+    for i in range(4):
+        at = slice(i * 256, i * 256 + 256)
+        s.acc_grad[:, at] = dot(s.in_full[at, :], s.gp_t[...]).T
+    unit_one, spread_one = standard(tok_ref[...].astype(F32))
+    grad_one = s.acc_grad[...]
+    s.vec_grad[4:5] = column_sum(grad_one * unit_one)
+    s.vec_grad[5:6] = column_sum(grad_one)
+    for i in range(8):
+        s.vec_send[i] = s.vec_grad[:, i * T : i * T + T]
+
+    def vec_to(dst):
+        return remote(s.vec_send.at[dst // 2], s.vec_recv.at[c], s.sem_vec, dst, c, (dst, f))
+
+    each_peer(lambda dst: vec_to(dst).start())
+    s.vec_recv[c] = s.vec_send[c // 2]
+    input_grad[...] = (
+        s.grad_middle[...] + standard_back(grad_one, row(4), unit_one, spread_one)
+    ).astype(LOW)
+
+    for copy in up_line:
+        copy.wait_recv()
+    up_sum = s.up_mine[z]
+    for k in range(3):
+        up_sum = up_sum + s.up_line[k].astype(F32)
+    s.up_piece[...] = up_sum.reshape(4, 32, 1024)
+    up_copies = []
+    for i in range(3):
+        for q in range(4):
+            copy = remote(
+                s.up_piece.at[plane_places[i], :, pl.ds(q * 256, 256)],
+                up_out.at[:, pl.ds(pl.multiple_of(q * 1024 + p * 256, 256), 256)],
+                s.sem_up,
+                i * 4 + q,
+                i * 4 + q,
+                planes[i],
+            )
+            copy.start()
+            up_copies.append(copy)
+    for q in range(4):
+        up_out[:, pl.ds(pl.multiple_of(q * 1024 + p * 256, 256), 256)] = s.up_piece[
+            p, :, q * 256 : q * 256 + 256
+        ]
+    for copy in down_line:
+        copy.wait_recv()
+    down_sum = s.down_mine[z]
+    for k in range(3):
+        down_sum = down_sum + s.down_line[k].astype(F32)
+    down_out[...] = down_sum
+    for copy in out_line:
+        copy.wait_recv()
+    out_sum = s.out_mine[z]
+    for k in range(3):
+        out_sum = out_sum + s.out_line[k].astype(F32)
+    out_out[...] = out_sum
+
+    def vec_arrived(src):
+        remote(
+            s.vec_send.at[src // 2], s.vec_recv.at[src], s.sem_vec, src, src, (src, f)
+        ).wait_recv()
+
+    each_peer(vec_arrived)
+    s.vec_mine[...] = jnp.sum(s.vec_recv[...], axis=0)
+    vec_pair = remote(s.vec_mine, s.vec_pair, s.sem_pair, 9, 9, sibling)
+    vec_pair.start()
+
+    def in_arrived(src):
+        remote(s.in_send.at[src], s.in_recv.at[src], s.sem_in, src, src, (src, f)).wait_recv()
+
+    each_peer(in_arrived)
+    for part in range(3):
+        for i in range(8):
+            pieces = [
+                s.in_recv[2 * i + w, :, part * 64 : part * 64 + 64].astype(F32)
+                for w in range(2)
+            ]
+            at = part * 1024 + i * T
+            in_out[:, at : at + T] = jnp.concatenate(pieces, axis=1)
+    vec_pair.wait()
+    vec_out[...] = s.vec_mine[...] + s.vec_pair[...]
+    for copy in up_copies:
+        copy.wait()
+    for copy in sent:
+        copy.wait_send()
+
+    def all_sent(dst):
+        back_copy(dst).wait_send()
+        grads_copy(dst).wait_send()
+        in_copy(dst).wait_send()
+        vec_to(dst).wait_send()
+
+    each_peer(all_sent)
+
+
+def body_fused(
+    tokens,
+    in_weight,
+    query_bias,
+    value_bias,
+    out_weight,
+    out_bias,
+    up_weight,
+    up_bias,
+    down_weight,
+    down_bias,
+    first_gain,
+    first_shift,
+    second_gain,
+    second_shift,
+    lengths,
+    slot_places,
+    cotangent,
+):
+    vectors = jnp.concatenate(
+        [
+            query_bias,
+            value_bias,
+            out_bias,
+            down_bias,
+            first_gain,
+            first_shift,
+            second_gain,
+            second_shift,
+            up_bias,
+        ]
+    )
+    vectors = vectors.astype(F32).reshape(12, 1, 512)
+    places = slot_places[0]
+    starts = jnp.cumsum(lengths[0]) - lengths[0]
+    first = jnp.max(jnp.where(starts[None, :] <= places[:, None], starts[None, :], 0), axis=1)
+    query_info = jnp.zeros((8, places.shape[0]), jnp.int32).at[0].set(places).at[1].set(first)
+    key_info = jnp.broadcast_to(places[:, None], (places.shape[0], T))
+    hbm = pl.BlockSpec(memory_space=pl.ANY)
+    vmem = pl.BlockSpec(memory_space=pltpu.VMEM)
+    outs = pl.pallas_call(
+        layer_kernel,
+        out_shape=(
+            jax.ShapeDtypeStruct((T, 1024), LOW),
+            jax.ShapeDtypeStruct((T, 1024), LOW),
+            jax.ShapeDtypeStruct((32, 3072), F32),
+            jax.ShapeDtypeStruct((32, 1024), F32),
+            jax.ShapeDtypeStruct((32, 4096), F32),
+            jax.ShapeDtypeStruct((128, 1024), F32),
+            jax.ShapeDtypeStruct((16, 128), F32),
+            jax.ShapeDtypeStruct((16, T, 1024), LOW),
+        ),
+        in_specs=[vmem] * 5 + [hbm] * 4,
+        out_specs=(vmem,) * 7 + (hbm,),
+        scratch_shapes=[scratch()],
+        compiler_params=pltpu.CompilerParams(
+            collective_id=0, has_side_effects=True, vmem_limit_bytes=60 * 2**20
+        ),
+        cost_estimate=pl.CostEstimate(
+            flops=16 * 10**9, bytes_accessed=40 * 2**20, transcendentals=10**7
+        ),
+    )(
+        tokens[0],
+        cotangent[0],
+        vectors,
+        key_info,
+        query_info,
+        in_weight,
+        out_weight,
+        up_weight,
+        down_weight,
+    )
+    layer_out, input_grad, in_grad, out_grad, up_grad, down_grad, vec = outs[:7]
+    index = lax.axis_index("ctx") * 2 + lax.axis_index("fsdp")
+    at = index % 4
+    small = lax.dynamic_slice(vec, (0, at * 32), (8, 32))
+    up_small = lax.dynamic_slice(vec, (8 + at, 0), (1, 128))[0]
+    return (
+        layer_out[None],
+        input_grad[None],
+        in_grad,
+        small[0],
+        small[1],
+        out_grad,
+        small[2],
+        up_grad,
+        up_small,
+        down_grad,
+        small[3],
+        small[4],
+        small[5],
+        small[6],
+        small[7],
+    )
+
+
 def solution(mesh):
     placed = (
         P("fsdp", "ctx", None),
@@ -345,7 +1219,7 @@
         P("fsdp", "ctx", None),
     )
     return jax.shard_map(
-        body,
+        body_fused if mesh.shape["ctx"] == H else body_general,
         mesh=mesh,
         in_specs=placed,
         out_specs=(

time: 1300 us -> 205 us (0.16)
  waiting for transfers between devices: 1030 us -> 0 us
  Pallas kernels: 0 us -> 177 us
  matrix products: 113 us -> 0 us
  blocking collectives: 62.3 us -> 0 us
  other arithmetic: 30.5 us -> 2.89 us
  local copies, waits for them, and re-layouts: 41.4 us -> 24 us
  between operations: 14.9 us -> 0.71 us
    reduce_scatter x5 -> x0, waiting for transfers between devices: 906 us -> none  [the longest x1 316 us: body(): lax.psum_scatter(terms.reshape(total_keys, 2 * width), 'ctx', scatter_dim...]
    pallas_call x0 -> x1, Pallas kernels: none -> 177 us  [body_fused(): pl.pallas_call(layer_kernel, out_shape=(jax.ShapeDtypeStruct((T, 1024), L...]
    all_gather x5 -> x0, waiting for transfers between devices: 121 us -> none  [the longest x1 104 us: body(): gathered = lax.all_gather(key_value, 'ctx', axis=0, tiled=True)]
    dot_general x19 -> x0, matrix products: 113 us -> none  [the longest x4 24.1 us: inner_rows(): jnp.einsum('tf,tg->fg', left, right, preferred_element_type=jnp.float32)]
    unnamed x1 -> x0, blocking collectives: 45.9 us -> none
    slice x5 -> x0, local copies, waits for them, and re-layouts: 23.3 us -> none  [the longest x2 12.9 us: split_pair(): pair[:, :width].reshape(size, H, HD)]
    concatenate x3 -> x0, other arithmetic: 17.8 us -> none  [the longest x1 10.7 us: body(): jnp.concatenate([in_grad_raw[:, :width] * scale, in_grad_raw[:, width:]],...]
    all_gather x9 -> x0, blocking collectives: 16.4 us -> none  [the longest x1 1.98 us: body(): lax.all_gather(down_bias, 'fsdp', axis=0, tiled=True)]
  transfers between devices with their start and end apart: 10 -> 0, of which waited for: 8 -> 0; matrix products, arithmetic and copies ran while one was open for 10% -> 0% of each run, Pallas kernels for 0% -> 0%
where the time goes in v2:
time: 205 us
  Pallas kernels  177 us (86%)
  local copies, waits for them, and re-layouts  24 us (12%)
  other arithmetic  2.89 us (1%)
    pallas_call x1, Pallas kernels, body_fused(): pl.pallas_call(layer_kernel, out_shape=(jax.ShapeDtypeStruct((T, 1024), L...  177 us
    unnamed x16, local copies, waits for them, and re-layouts  17.9 us

profile of v2, /device:TPU:0, one launch (start us, length us, event | category | flops | bytes accessed | tf_op | source)
XLA Modules:
  0.0 204.5 jit_solution(7931918652503945433)
XLA Ops:
  0.7 0.9 dynamic-update-slice.6
  1.5 0.9 dynamic-update-slice.7
  2.4 0.9 dynamic-update-slice.8
  3.2 0.9 dynamic-update-slice.9
  4.1 0.9 dynamic-update-slice.10
  5.0 0.9 dynamic-update-slice.11
  5.8 0.9 dynamic-update-slice.12
  6.7 0.9 dynamic-update-slice.13
  7.5 0.7 constant_dynamic-update-slice_fusion
  8.2 0.6 convert_element_type.15
  8.8 2.0 broadcast_in_dim.27.key_ref
  10.8 0.7 scatter.6
  11.6 0.8 reduce-window_clone.1
  12.4 0.7 subtract_bitcast_fusion
  13.0 0.8 fusion
  13.8 0.2 scatter.9.query_ref
  14.0 0.0 copy-start
  14.1 0.6 copy-done
  14.7 176.9 %shard_map.280 = (bf16[128,1024]{1,0:T(8,128)(2,1)}, bf16[128,1024]{1,0:T(8,128)(2,1)}, f32[32,3072]{1,0:T(8,128)}, f32[32,1024]{1,0:T(8,128)}, f32[32,4096]{1,0...) custom-call(bf16[128,1024]{1,0:T(8,128)(2,1)} %bitcast.33, ...), custom_call_target="tpu_custom_call" | custom-call | flops 16000000000 | bytes 41943040 | tf_op jit(solution)/shard_map/pallas_call | solution.py:1145
  191.6 0.8 constant_dynamic-slice_fusion
  192.4 0.5 slice_bitcast_fusion
  192.9 1.2 dynamic-slice_bitcast_fusion
  194.1 1.7 copy.48
  195.8 1.7 copy.49
  197.5 1.8 copy.50
  199.2 1.6 copy.51
  200.8 1.9 copy.52
  202.7 1.9 copy.53
  (1 shorter events, 0.0 us)
Async XLA Ops:
  14.0 0.6 copy-start

commit v3 on v2

--- a/solution.py
+++ b/solution.py
@@ -384,6 +384,8 @@
 class Scratch(NamedTuple):
     vec: Any
     bias: Any
+    key: Any
+    query: Any
     in_full: Any
     out_full: Any
     up_full: Any
@@ -408,11 +410,12 @@
     acc_out: Any
     acc_grad: Any
     grad_hidden: Any
-    vec_grad: Any
+    early_grad: Any
+    late_grad: Any
+    dq: Any
     do_t: Any
     q_rows: Any
     do_rows: Any
-    dkv: Any
     down_mine: Any
     down_theirs: Any
     down_pair: Any
@@ -433,8 +436,10 @@
     in_pair: Any
     in_send: Any
     in_recv: Any
-    vec_send: Any
-    vec_recv: Any
+    early_send: Any
+    early_recv: Any
+    late_send: Any
+    late_recv: Any
     vec_mine: Any
     vec_pair: Any
     sem_load: Any
@@ -452,7 +457,10 @@
     sem_grads: Any
     sem_up: Any
     sem_in: Any
-    sem_vec: Any
+    sem_early: Any
+    sem_late: Any
+    sem_dq: Any
+    sem_in_w: Any
     sem_one_load: Any
 
 
@@ -466,6 +474,8 @@
     return Scratch(
         vec=v((2, 12, 1, 512), F32),
         bias=v((2, 1, 1024), F32),
+        key=v((2048, 128), F32),
+        query=v((8, 2048), F32),
         in_full=v((1024, 3072), LOW),
         out_full=v((1024, 1024), LOW),
         up_full=v((1024, 4096), LOW),
@@ -490,11 +500,12 @@
         acc_out=v((128, 1024), F32),
         acc_grad=v((128, 1024), F32),
         grad_hidden=v((512, 1024), LOW),
-        vec_grad=v((16, 1024), F32),
+        early_grad=v((8, 1024), F32),
+        late_grad=v((8, 1024), F32),
+        dq=v((64, 2048), F32),
         do_t=v((64, 2048), LOW),
         q_rows=v((2048, 128), LOW),
         do_rows=v((2048, 128), LOW),
-        dkv=v((2048, 128), F32),
         down_mine=v((4, 128, 1024), F32),
         down_theirs=v((4, 128, 1024), LOW),
         down_pair=v((4, 128, 1024), LOW),
@@ -510,15 +521,17 @@
         out_line=v((3, 32, 1024), LOW),
         dqkv=v((16, 192, 128), LOW),
         gp_t=v((3072, 128), LOW),
-        in_mine=v((16, 32, 256), F32),
-        in_theirs=v((16, 32, 256), LOW),
-        in_pair=v((16, 32, 256), LOW),
-        in_send=v((16, 32, 256), LOW),
-        in_recv=v((16, 32, 256), LOW),
-        vec_send=v((8, 16, 128), F32),
-        vec_recv=v((16, 16, 128), F32),
-        vec_mine=v((16, 128), F32),
-        vec_pair=v((16, 128), F32),
+        in_mine=v((16, 48, 128), F32),
+        in_theirs=v((16, 48, 128), LOW),
+        in_pair=v((16, 48, 128), LOW),
+        in_send=v((16, 48, 128), LOW),
+        in_recv=v((16, 48, 128), LOW),
+        early_send=v((8, 8, 128), F32),
+        early_recv=v((16, 8, 128), F32),
+        late_send=v((8, 8, 128), F32),
+        late_recv=v((16, 8, 128), F32),
+        vec_mine=v((24, 128), F32),
+        vec_pair=v((24, 128), F32),
         sem_load=sems(6),
         sem_pair=sems(10),
         sem_qkv=sems(16),
@@ -534,7 +547,10 @@
         sem_grads=sems(16),
         sem_up=sems(12),
         sem_in=sems(16),
-        sem_vec=sems(16),
+        sem_early=sems(16),
+        sem_late=sems(16),
+        sem_dq=sems(16),
+        sem_in_w=sems(12),
         sem_one_load=pltpu.SemaphoreType.DMA((16,)),
     )
 
@@ -542,23 +558,13 @@
 def layer_kernel(
     tok_ref,
     cot_ref,
-    vec_ref,
-    key_ref,
-    query_ref,
-    in_hbm,
-    out_hbm,
-    up_hbm,
-    down_hbm,
-    layer_out,
-    input_grad,
-    in_out,
-    out_out,
-    up_out,
-    down_out,
-    vec_out,
-    one_hbm,
-    s,
+    place_ref,
+    length_ref,
+    *rest,
 ):
+    vec_refs, rest = rest[:9], rest[9:]
+    in_hbm, out_hbm, up_hbm, down_hbm = rest[:4]
+    layer_out, input_grad, in_out, out_out, up_out, down_out, vec_out, one_hbm, s = rest[4:]
     n = 16
     scale = HD ** (-0.5)
     c, f = lax.axis_index("ctx"), lax.axis_index("fsdp")
@@ -568,7 +574,8 @@
     sibling = (c, 1 - f)
     plane_places = [2 * y + 1 - x, 2 * (1 - y) + x, 2 * (1 - y) + 1 - x]
     planes = [(home + place, f) for place in plane_places]
-    z_peers = [((z + k) % 4) for k in range(1, 4)]
+    near = z + 1 - 2 * (z % 2)
+    far = (z + 2) % 4
     first_core = f == 0
 
     def remote(src, dst, sems, i, j, device):
@@ -603,37 +610,57 @@
 
     each_peer(greet)
     pl.semaphore_signal(barrier, inc=1, device_id=sibling, device_id_type=MESH_ID)
+    for i in range(8):
+        s.vec[f, i] = vec_refs[i][...].astype(F32).reshape(1, 512)
+    for i in range(4):
+        s.vec[f, 8 + i] = vec_refs[8][i * 512 : i * 512 + 512].astype(F32).reshape(1, 512)
+    in_load = pltpu.make_async_copy(in_hbm, s.in_full.at[pl.ds(f * 512, 512)], s.sem_load.send.at[0])
+    in_load.start()
+    pl.semaphore_wait(barrier, n)
+    vec_copy = remote(s.vec.at[f], s.vec.at[f], s.sem_pair, 4, 4, sibling)
+    vec_copy.start()
+
+    def in_copy_of(g, part):
+        at = pl.ds(pl.multiple_of(part * 1024 + (z + g) % 4 * 256, 256), 256)
+        return remote(
+            in_hbm.at[:, at],
+            s.in_full.at[pl.ds(f * 512, 512), at],
+            s.sem_in_w,
+            g * 3 + part,
+            g * 3 + part,
+            sibling,
+        )
+
+    for g in range(4):
+        for part in range(3):
+            in_copy_of(g, part).start()
+    sent = [vec_copy]
+    cot_copies = to_planes(lambda i: cot_ref, s.cot_all, s.sem_cot)
+    sent += cot_copies
+
     weights = [
-        (in_hbm, s.in_full, 512),
         (out_hbm, s.out_full, 512),
         (up_hbm, s.up_full, 512),
         (down_hbm, s.down_full, 2048),
     ]
-    loads, pairs = [], []
+    loads, pairs = [None], [None]
     for i, (src, dst, size) in enumerate(weights):
-        load = pltpu.make_async_copy(src, dst.at[pl.ds(f * size, size)], s.sem_load.send.at[i])
-        load.start()
+        load = pltpu.make_async_copy(src, dst.at[pl.ds(f * size, size)], s.sem_load.send.at[1 + i])
         loads.append(load)
-    s.vec[f] = vec_ref[...]
-    pl.semaphore_wait(barrier, n)
-    vec_copy = remote(vec_ref, s.vec.at[f], s.sem_pair, 4, 4, sibling)
-    vec_copy.start()
-    for i, (src, dst, size) in enumerate(weights):
-        pair = remote(src, dst.at[pl.ds(f * size, size)], s.sem_pair, i, i, sibling)
-        pair.start()
+        pair = remote(src, dst.at[pl.ds(f * size, size)], s.sem_pair, 1 + i, 1 + i, sibling)
         pairs.append(pair)
-    sent = [vec_copy] + pairs
+    sent += pairs[1:]
 
     def row(i):
         return jnp.concatenate([s.vec[0, i], s.vec[1, i]], axis=1)
 
     unit_one, unused = standard(tok_ref[...].astype(F32))
+    s.cot_all[0] = cot_ref[...]
     vec_copy.wait_recv()
     s.normed_one[...] = (unit_one * row(4) + row(5)).astype(LOW)
     s.bias[0] = row(0)
     s.bias[1] = row(1)
-    loads[0].wait()
-    pairs[0].wait_recv()
+    in_load.wait()
 
     def qkv_copy(dst):
         return remote(
@@ -643,6 +670,7 @@
     def project(g, carry):
         group = (z + g) % 4
         for part in range(3):
+            in_copy_of(g, part).wait_recv()
             at = pl.ds(pl.multiple_of(part * 1024 + group * 256, 256), 256)
             acc = dot(s.normed_one[...], s.in_full[:, at])
             if part == 0:
@@ -669,15 +697,22 @@
         return carry
 
     lax.fori_loop(0, 4, project, 0)
+    for i in range(1, 4):
+        loads[i].start()
+        pairs[i].start()
     keep = pltpu.make_async_copy(s.normed_one, one_hbm.at[c], s.sem_load.send.at[4])
     keep.start()
-    for k in range(3):
-        copy = remote(s.normed_one, one_hbm.at[c], s.sem_one, k, c, (z_peers[k] * 4 + p, f))
-        copy.start()
-        sent.append(copy)
-    s.cot_all[0] = cot_ref[...]
-    cot_copies = to_planes(lambda i: cot_ref, s.cot_all, s.sem_cot)
-    sent += cot_copies
+
+    place = place_ref[...]
+    first, begun = jnp.zeros((1, 2048), jnp.int32), 0
+    for i in range(length_ref.shape[1]):
+        first = jnp.where(place >= begun, begun, first)
+        begun = begun + length_ref[0, i]
+    s.query[0:1] = place.astype(F32)
+    s.query[1:2] = first.astype(F32)
+    for i in range(n):
+        at = slice(i * T, i * T + T)
+        s.key[at] = jnp.broadcast_to(s.query[0:1, at], (T, T)).T
 
     def qkv_arrived(src):
         remote(
@@ -686,14 +721,30 @@
 
     each_peer(qkv_arrived)
 
+    def one_copy(slot, sems, i, device):
+        return remote(one_hbm.at[slot], one_hbm.at[slot], Sems(sems.send, s.sem_one.recv), i, slot, device)
+
+    keep.wait()
+    far_slot = far * 4 + p
+    one_far = one_copy(c, s.sem_one, 0, (far_slot, f))
+    one_far.start()
+    sent.append(one_far)
+
+    def relay(k, slot):
+        for i in range(3):
+            copy = one_copy(slot, s.sem_relay, k * 3 + i, planes[i])
+            copy.start()
+            sent.append(copy)
+
+
     for i in range(n):
         at = slice(i * T, i * T + T)
         s.kv[at] = turned(s.qkv_t[64:192, at]).astype(LOW)
     nothing = jnp.zeros((64, 256), LOW)
 
     def seen(keys, at):
-        place = jnp.concatenate([key_ref[keys], key_ref[keys]], axis=1)
-        return (place >= query_ref[1:2, at]) & (place <= query_ref[0:1, at])
+        place = jnp.concatenate([s.key[keys], s.key[keys]], axis=1)
+        return (place >= s.query[1:2, at]) & (place <= s.query[0:1, at])
 
     def head_copy(dst):
         return remote(s.send_head.at[dst], s.att_t.at[p * 4 + z], s.sem_head, dst, c, (dst, f))
@@ -741,6 +792,16 @@
         remote(s.send_head.at[src], s.att_t.at[slot], s.sem_head, src, src, (src, f)).wait_recv()
 
     each_peer(head_arrived)
+
+    def one_arrived(slot):
+        one_copy(slot, s.sem_one, 0, (slot, f)).wait_recv()
+
+    one_arrived(far_slot)
+    near_device = (near * 4 + p, f)
+    for i, slot in enumerate((c, far_slot)):
+        copy = one_copy(slot, s.sem_one, 1 + i, near_device)
+        copy.start()
+        sent.append(copy)
     s.att_all[0] = s.att_t[pl.ds(p * 4, 4)]
     att_copies = to_planes(
         lambda i: s.att_t.at[pl.ds(plane_places[i] * 4, 4)], s.att_all, s.sem_att
@@ -764,7 +825,7 @@
         pairs[i].wait_recv()
     s.acc_out[...] = jnp.zeros((T, 1024), F32)
     s.acc_grad[...] = jnp.zeros((T, 1024), F32)
-    s.vec_grad[...] = jnp.zeros((16, 1024), F32)
+    s.late_grad[...] = jnp.zeros((8, 1024), F32)
 
     def feed(j, carry):
         at = lanes(j, 512)
@@ -776,22 +837,22 @@
         s.acc_grad[...] += dot_nt(grad_hidden, s.up_full[:, at])
         summed = column_sum(grad_hidden.astype(F32))
         for q in range(4):
-            s.vec_grad[8 + q : 9 + q, lanes(j, T)] = summed[:, q * T : q * T + T]
+            s.early_grad[4 + q : 5 + q, lanes(j, T)] = summed[:, q * T : q * T + T]
         return carry
 
     lax.fori_loop(0, 8, feed, 0)
     layer_out[...] = (s.middle[...] + s.acc_out[...] + row(3)).astype(LOW)
     grad_result = cot_ref[...].astype(F32)
-    s.vec_grad[3:4] = column_sum(grad_result)
+    s.early_grad[1:2] = column_sum(grad_result)
     unit_two, spread_two = standard(s.middle[...])
     grad_two = s.acc_grad[...]
-    s.vec_grad[6:7] = column_sum(grad_two * unit_two)
-    s.vec_grad[7:8] = column_sum(grad_two)
+    s.early_grad[2:3] = column_sum(grad_two * unit_two)
+    s.early_grad[3:4] = column_sum(grad_two)
     grad_middle = grad_result + standard_back(grad_two, row(6), unit_two, spread_two)
     s.grad_middle[...] = grad_middle
     branch = grad_middle.astype(LOW)
     s.branch_all[0] = branch
-    s.vec_grad[2:3] = column_sum(branch.astype(F32))
+    s.early_grad[0:1] = column_sum(branch.astype(F32))
 
     def head_done(dst):
         head_copy(dst).wait_send()
@@ -810,25 +871,29 @@
     branch_copies = to_planes(lambda i: s.branch_all.at[0], s.branch_all, s.sem_branch)
     sent += branch_copies
 
-    def one_arrived(src):
-        remote(s.normed_one, one_hbm.at[src], s.sem_one, 0, src, (src, f)).wait_recv()
-
-    keep.wait()
-    for k in range(3):
-        one_arrived(z_peers[k] * 4 + p)
-    for k in range(4):
-        slot = (c if k == 0 else z_peers[k - 1] * 4 + p)
-        for i in range(3):
-            copy = pltpu.make_async_remote_copy(
-                src_ref=one_hbm.at[slot],
-                dst_ref=one_hbm.at[slot],
-                send_sem=s.sem_relay.send.at[k * 3 + i],
-                recv_sem=s.sem_one.recv.at[slot],
-                device_id=planes[i],
-                device_id_type=MESH_ID,
-            )
-            copy.start()
-            sent.append(copy)
+    def to_owners(grad, send, recv, sems):
+        def copy_to(dst):
+            return remote(send.at[dst // 2], recv.at[c], sems, dst, c, (dst, f))
+
+        for i in range(8):
+            send[i] = grad[:, i * T : i * T + T]
+        each_peer(lambda dst: copy_to(dst).start())
+        recv[c] = send[c // 2]
+        return copy_to
+
+    def from_owners(send, recv, sems):
+        each_peer(
+            lambda src: remote(
+                send.at[src // 2], recv.at[src], sems, src, src, (src, f)
+            ).wait_recv()
+        )
+        return jnp.sum(recv[...], axis=0)
+
+    near_slots = (near * 4 + p, (near + 2) % 4 * 4 + p)
+    for slot in near_slots:
+        one_arrived(slot)
+    for k, slot in enumerate((c, far_slot) + near_slots):
+        relay(k, slot)
 
     for i in range(3):
         cot_copies[i].wait_recv()
@@ -870,28 +935,116 @@
     up_pair = remote(s.up_theirs, s.up_pair, s.sem_pair, 6, 6, sibling)
     up_pair.start()
 
-    def to_line(mine, theirs, pair, line, base):
+    def to_near(mine, theirs, pair, line, base):
         copies = []
-        for k in range(3):
-            at = z_peers[k]
-            theirs[at] = (
-                mine[at] + pair[at].astype(F32)
-            ).astype(LOW)
+        for j in range(2):
+            at = (near + 2 * j) % 4
+            theirs[at] = (mine[at] + pair[at].astype(F32)).astype(LOW)
             copy = remote(
-                theirs.at[at],
-                line.at[k],
-                s.sem_line,
-                base + k,
-                base + k,
-                (at * 4 + p, f),
+                theirs.at[at], line.at[j], s.sem_line, base + j, base + j, (near * 4 + p, f)
             )
             copy.start()
             copies.append(copy)
-        mine[z] += pair[z].astype(F32)
+        for at in (z, far):
+            mine[at] += pair[at].astype(F32)
         return copies
 
+    def to_far(mine, theirs, line, base, copies):
+        for copy in copies:
+            copy.wait_recv()
+        mine[z] += line[0].astype(F32)
+        theirs[far] = (mine[far] + line[1].astype(F32)).astype(LOW)
+        copy = remote(
+            theirs.at[far], line.at[2], s.sem_line, base + 2, base + 2, (far_slot, f)
+        )
+        copy.start()
+        return copies + [copy]
+
     down_pair.wait()
-    down_line = to_line(s.down_mine, s.down_theirs, s.down_pair, s.down_line, 0)
+    down_line = to_near(s.down_mine, s.down_theirs, s.down_pair, s.down_line, 0)
+    up_pair.wait()
+    up_line = to_near(s.up_mine, s.up_theirs, s.up_pair, s.up_line, 3)
+    early_to = to_owners(s.early_grad, s.early_send, s.early_recv, s.sem_early)
+
+    def qkv_done(dst):
+        qkv_copy(dst).wait_send()
+
+    each_peer(qkv_done)
+
+    def back_arrived(src):
+        remote(
+            s.send_head.at[src], s.do_t.at[:, lanes(src, T)], s.sem_back, src, src, (src, f)
+        ).wait_recv()
+
+    each_peer(back_arrived)
+    small_nothing = jnp.zeros((64, T), LOW)
+    for i in range(n):
+        at = slice(i * T, i * T + T)
+        s.q_rows[at] = turned(
+            jnp.concatenate([s.qkv_t[0:64, at], small_nothing], axis=0)
+        ).astype(LOW)
+        s.do_rows[at] = turned(
+            jnp.concatenate([small_nothing, s.do_t[:, at]], axis=0)
+        ).astype(LOW)
+    s.delta[...] = column_sum(s.do_t[...].astype(F32) * s.head_out[...])
+    s.dq[...] = jnp.zeros((64, 2048), F32)
+
+    def grads_copy(dst):
+        return remote(
+            s.send_qkv.at[dst, pl.ds(64, 128)],
+            s.dqkv.at[c, pl.ds(64, 128)],
+            s.sem_grads,
+            dst,
+            c,
+            (dst, f),
+        )
+
+    def dq_copy(dst):
+        return remote(
+            s.send_qkv.at[dst, pl.ds(0, 64)],
+            s.dqkv.at[c, pl.ds(0, 64)],
+            s.sem_dq,
+            dst,
+            c,
+            (dst, f),
+        )
+
+    def backward(i, carry):
+        block = (c // 2 + i) % 8
+        keys = pl.ds(pl.multiple_of(block * 256, 256), 256)
+        key_t = s.qkv_t[64:128, keys]
+        both = s.kv[keys]
+        dkv = jnp.zeros((256, 128), F32)
+        for q in range(8):
+            at = slice(q * 256, q * 256 + 256)
+            query = jnp.concatenate([s.qkv_t[0:64, at], nothing], axis=0)
+            grad = jnp.concatenate([nothing, s.do_t[:, at]], axis=0)
+            score = dot(both, query)
+            prob = jnp.where(seen(keys, at), jnp.exp(score - s.lse[:, at]), 0.0)
+            grad_prob = dot(both, grad)
+            grad_score = (prob * (grad_prob - s.delta[:, at])).astype(LOW)
+            dkv = dkv + (
+                dot(grad_score, s.q_rows[at]) + dot(prob.astype(LOW), s.do_rows[at])
+            )
+            s.dq[:, at] += dot(key_t, grad_score)
+        for u in range(2):
+            dst = block * 2 + u
+            s.send_qkv[dst, 64:192] = dkv[u * T : u * T + T].T.astype(LOW)
+
+            @pl.when(dst != c)
+            def _():
+                grads_copy(dst).start()
+
+        return carry
+
+    lax.fori_loop(0, 4, backward, 0)
+    down_line = to_far(s.down_mine, s.down_theirs, s.down_line, 0, down_line)
+    lax.fori_loop(4, 8, backward, 0)
+    for i in range(n):
+        s.send_qkv[i, 0:64] = s.dq[:, i * T : i * T + T].astype(LOW)
+    each_peer(lambda dst: dq_copy(dst).start())
+    s.dqkv[c] = s.send_qkv[c]
+    up_line = to_far(s.up_mine, s.up_theirs, s.up_line, 3, up_line)
     for i in range(3):
         att_copies[i].wait_recv()
         branch_copies[i].wait_recv()
@@ -903,70 +1056,12 @@
     s.out_theirs[...] = theirs
     out_pair = remote(s.out_theirs, s.out_pair, s.sem_pair, 7, 7, sibling)
     out_pair.start()
-    up_pair.wait()
-    up_line = to_line(s.up_mine, s.up_theirs, s.up_pair, s.up_line, 3)
     out_pair.wait()
-    out_line = to_line(s.out_mine, s.out_theirs, s.out_pair, s.out_line, 6)
-    sent += down_line + up_line + out_line
-
-    def qkv_done(dst):
-        qkv_copy(dst).wait_send()
-
-    each_peer(qkv_done)
-
-    def back_arrived(src):
-        remote(
-            s.send_head.at[src], s.do_t.at[:, lanes(src, T)], s.sem_back, src, src, (src, f)
-        ).wait_recv()
-
-    each_peer(back_arrived)
-    small_nothing = jnp.zeros((64, T), LOW)
-    for i in range(n):
-        at = slice(i * T, i * T + T)
-        s.q_rows[at] = turned(
-            jnp.concatenate([s.qkv_t[0:64, at], small_nothing], axis=0)
-        ).astype(LOW)
-        s.do_rows[at] = turned(
-            jnp.concatenate([small_nothing, s.do_t[:, at]], axis=0)
-        ).astype(LOW)
-    s.delta[...] = column_sum(s.do_t[...].astype(F32) * s.head_out[...])
-    s.dkv[...] = jnp.zeros((2048, 128), F32)
-
-    def backward(block, carry):
-        at = lanes(block, 256)
-        query = jnp.concatenate([s.qkv_t[0:64, at], nothing], axis=0)
-        grad = jnp.concatenate([nothing, s.do_t[:, at]], axis=0)
-        lse, delta = s.lse[:, at], s.delta[:, at]
-        dq = jnp.zeros((64, 256), F32)
-        for k in range(8):
-            keys = slice(k * 256, k * 256 + 256)
-            score = dot(s.kv[keys], query)
-            prob = jnp.where(seen(keys, at), jnp.exp(score - lse), 0.0)
-            grad_prob = dot(s.kv[keys], grad)
-            grad_score = (prob * (grad_prob - delta)).astype(LOW)
-            s.dkv[keys] += dot(grad_score, s.q_rows[at]) + dot(
-                prob.astype(LOW), s.do_rows[at]
-            )
-            dq = dq + dot(s.qkv_t[64:128, keys], grad_score)
-        for u in range(2):
-            s.send_qkv[block * 2 + u, 0:64] = dq[:, u * T : u * T + T].astype(LOW)
-        return carry
-
-    lax.fori_loop(0, 8, backward, 0)
-
-    def grads_copy(dst):
-        return remote(s.send_qkv.at[dst], s.dqkv.at[c], s.sem_grads, dst, c, (dst, f))
-
-    for i in range(n):
-        s.send_qkv[i, 64:192] = s.dkv[i * T : i * T + T].T.astype(LOW)
-    each_peer(lambda dst: grads_copy(dst).start())
-    s.dqkv[c] = s.send_qkv[c]
+    out_line = to_near(s.out_mine, s.out_theirs, s.out_pair, s.out_line, 6)
 
     for k in range(4):
-        base = (z + k) % 4 * 4
         for i in range(3):
-            one_arrived(base + plane_places[i])
-    one_full = s.down_full.at[pl.ds(0, 2048)]
+            one_arrived((z + k) % 4 * 4 + plane_places[i])
     one_loads = []
     for i in range(n):
         load = pltpu.make_async_copy(
@@ -977,6 +1072,13 @@
     for load in one_loads:
         load.wait()
     head_grad = jnp.concatenate([s.send_qkv[i] for i in range(n)], axis=1)
+    bias_sums = dot_nt(jnp.ones((8, 2048), LOW), head_grad)
+    s.vec_mine[16:24] = jnp.concatenate([bias_sums[:, 0:64] * scale, bias_sums[:, 128:192]], axis=1)
+
+    def packed(rows):
+        tail = jnp.concatenate([rows[:, 0:16, 128:192], rows[:, 16:32, 128:192]], axis=2)
+        return jnp.concatenate([rows[:, :, 0:128], tail], axis=1)
+
     for i in range(4):
         part = dot(head_grad, s.down_full[0:2048, i * 256 : i * 256 + 256])
         part = jnp.concatenate(
@@ -985,13 +1087,30 @@
         for u in range(2):
             parts = part[:, u * T : u * T + T].T.reshape(2, 2, 32, 256)
             at = slice(4 * i + 2 * u, 4 * i + 2 * u + 2)
-            s.in_mine[at] = jnp.where(first_core, parts[:, 0], parts[:, 1])
-            s.in_theirs[at] = jnp.where(first_core, parts[:, 1], parts[:, 0]).astype(LOW)
+            s.in_mine[at] = packed(jnp.where(first_core, parts[:, 0], parts[:, 1]))
+            s.in_theirs[at] = packed(jnp.where(first_core, parts[:, 1], parts[:, 0])).astype(LOW)
     in_pair = remote(s.in_theirs, s.in_pair, s.sem_pair, 8, 8, sibling)
     in_pair.start()
 
     def grads_arrived(src):
-        remote(s.send_qkv.at[src], s.dqkv.at[src], s.sem_grads, src, src, (src, f)).wait_recv()
+        remote(
+            s.send_qkv.at[src, pl.ds(64, 128)],
+            s.dqkv.at[src, pl.ds(64, 128)],
+            s.sem_grads,
+            src,
+            src,
+            (src, f),
+        ).wait_recv()
+
+    def dq_arrived(src):
+        remote(
+            s.send_qkv.at[src, pl.ds(0, 64)],
+            s.dqkv.at[src, pl.ds(0, 64)],
+            s.sem_dq,
+            src,
+            src,
+            (src, f),
+        ).wait_recv()
 
     in_pair.wait()
     s.in_send[...] = (s.in_mine[...] + s.in_pair[...].astype(F32)).astype(LOW)
@@ -1003,36 +1122,29 @@
     s.in_recv[c] = s.in_send[c]
     each_peer(grads_arrived)
     for h in range(n):
-        s.gp_t[h * 64 : h * 64 + 64] = s.dqkv[h, 0:64] * jnp.asarray(scale, LOW)
         s.gp_t[1024 + h * 64 : 1088 + h * 64] = s.dqkv[h, 64:128]
         s.gp_t[2048 + h * 64 : 2112 + h * 64] = s.dqkv[h, 128:192]
-    ones = jnp.ones((8, T), LOW)
-    s.vec_grad[0:1] = dot_nt(ones, s.gp_t[0:1024])[0:1]
-    s.vec_grad[1:2] = dot_nt(ones, s.gp_t[2048:3072])[0:1]
     for i in range(4):
         at = slice(i * 256, i * 256 + 256)
-        s.acc_grad[:, at] = dot(s.in_full[at, :], s.gp_t[...]).T
+        s.acc_grad[:, at] = dot(s.in_full[at, 1024:3072], s.gp_t[1024:3072]).T
+    each_peer(dq_arrived)
+    for h in range(n):
+        s.gp_t[h * 64 : h * 64 + 64] = s.dqkv[h, 0:64] * jnp.asarray(scale, LOW)
+    for i in range(4):
+        at = slice(i * 256, i * 256 + 256)
+        s.acc_grad[:, at] += dot(s.in_full[at, 0:1024], s.gp_t[0:1024]).T
     unit_one, spread_one = standard(tok_ref[...].astype(F32))
     grad_one = s.acc_grad[...]
-    s.vec_grad[4:5] = column_sum(grad_one * unit_one)
-    s.vec_grad[5:6] = column_sum(grad_one)
-    for i in range(8):
-        s.vec_send[i] = s.vec_grad[:, i * T : i * T + T]
-
-    def vec_to(dst):
-        return remote(s.vec_send.at[dst // 2], s.vec_recv.at[c], s.sem_vec, dst, c, (dst, f))
-
-    each_peer(lambda dst: vec_to(dst).start())
-    s.vec_recv[c] = s.vec_send[c // 2]
+    s.late_grad[0:1] = column_sum(grad_one * unit_one)
+    s.late_grad[1:2] = column_sum(grad_one)
+    late_to = to_owners(s.late_grad, s.late_send, s.late_recv, s.sem_late)
     input_grad[...] = (
         s.grad_middle[...] + standard_back(grad_one, row(4), unit_one, spread_one)
     ).astype(LOW)
 
-    for copy in up_line:
-        copy.wait_recv()
-    up_sum = s.up_mine[z]
-    for k in range(3):
-        up_sum = up_sum + s.up_line[k].astype(F32)
+    out_line = to_far(s.out_mine, s.out_theirs, s.out_line, 6, out_line)
+    up_line[2].wait_recv()
+    up_sum = s.up_mine[z] + s.up_line[2].astype(F32)
     s.up_piece[...] = up_sum.reshape(4, 32, 1024)
     up_copies = []
     for i in range(3):
@@ -1051,26 +1163,13 @@
         up_out[:, pl.ds(pl.multiple_of(q * 1024 + p * 256, 256), 256)] = s.up_piece[
             p, :, q * 256 : q * 256 + 256
         ]
-    for copy in down_line:
-        copy.wait_recv()
-    down_sum = s.down_mine[z]
-    for k in range(3):
-        down_sum = down_sum + s.down_line[k].astype(F32)
-    down_out[...] = down_sum
-    for copy in out_line:
-        copy.wait_recv()
-    out_sum = s.out_mine[z]
-    for k in range(3):
-        out_sum = out_sum + s.out_line[k].astype(F32)
-    out_out[...] = out_sum
-
-    def vec_arrived(src):
-        remote(
-            s.vec_send.at[src // 2], s.vec_recv.at[src], s.sem_vec, src, src, (src, f)
-        ).wait_recv()
-
-    each_peer(vec_arrived)
-    s.vec_mine[...] = jnp.sum(s.vec_recv[...], axis=0)
+    down_line[2].wait_recv()
+    down_out[...] = s.down_mine[z] + s.down_line[2].astype(F32)
+    out_line[2].wait_recv()
+    out_out[...] = s.out_mine[z] + s.out_line[2].astype(F32)
+
+    s.vec_mine[0:8] = from_owners(s.early_send, s.early_recv, s.sem_early)
+    s.vec_mine[8:16] = from_owners(s.late_send, s.late_recv, s.sem_late)
     vec_pair = remote(s.vec_mine, s.vec_pair, s.sem_pair, 9, 9, sibling)
     vec_pair.start()
 
@@ -1078,28 +1177,53 @@
         remote(s.in_send.at[src], s.in_recv.at[src], s.sem_in, src, src, (src, f)).wait_recv()
 
     each_peer(in_arrived)
-    for part in range(3):
-        for i in range(8):
-            pieces = [
-                s.in_recv[2 * i + w, :, part * 64 : part * 64 + 64].astype(F32)
-                for w in range(2)
-            ]
-            at = part * 1024 + i * T
-            in_out[:, at : at + T] = jnp.concatenate(pieces, axis=1)
+    for i in range(8):
+        a, b = s.in_recv[2 * i].astype(F32), s.in_recv[2 * i + 1].astype(F32)
+        at = i * T
+        in_out[:, at : at + T] = jnp.concatenate([a[0:32, 0:64], b[0:32, 0:64]], axis=1)
+        at = 1024 + i * T
+        in_out[:, at : at + T] = jnp.concatenate([a[0:32, 64:T], b[0:32, 64:T]], axis=1)
+        at = 2048 + i * T
+        in_out[0:16, at : at + T] = jnp.concatenate([a[32:48, 0:64], b[32:48, 0:64]], axis=1)
+        in_out[16:32, at : at + T] = jnp.concatenate([a[32:48, 64:T], b[32:48, 64:T]], axis=1)
     vec_pair.wait()
-    vec_out[...] = s.vec_mine[...] + s.vec_pair[...]
+    total = s.vec_mine[...] + s.vec_pair[...]
+    place = (c * 2 + f) % 4
+    picked, up_row = total[0:16, 0:32], total[4:5]
+    for i in range(1, 4):
+        picked = jnp.where(place == i, total[0:16, 32 * i : 32 * i + 32], picked)
+        up_row = jnp.where(place == i, total[4 + i : 5 + i], up_row)
+    vec_out[0:16, 0:32] = picked
+    vec_out[16:24, 0:32] = jnp.where(first_core, total[16:24, 0:32], total[16:24, 32:64])
+    vec_out[24:32, 0:32] = jnp.where(first_core, total[16:24, 64:96], total[16:24, 96:128])
+    vec_out[32:40] = jnp.broadcast_to(up_row, (8, T))
     for copy in up_copies:
         copy.wait()
+    for g in range(4):
+        for part in range(3):
+            in_copy_of(g, part).wait_send()
+    sent += [copy for line in (down_line, up_line, out_line) for copy in line]
     for copy in sent:
         copy.wait_send()
 
     def all_sent(dst):
         back_copy(dst).wait_send()
         grads_copy(dst).wait_send()
+        dq_copy(dst).wait_send()
         in_copy(dst).wait_send()
-        vec_to(dst).wait_send()
+        early_to(dst).wait_send()
+        late_to(dst).wait_send()
 
     each_peer(all_sent)
+
+
+def finish_kernel(*refs):
+    vec = refs[6]
+    for src, dst in zip(refs[:6], refs[7:13]):
+        dst[...] = src[...]
+    for i, dst in zip((16, 24, 0, 1, 8, 9, 2, 3), refs[13:21]):
+        dst[...] = vec[i : i + 1, 0:32].reshape(32)
+    refs[21][...] = vec[32:33].reshape(T)
 
 
 def body_fused(
@@ -1121,25 +1245,17 @@
     slot_places,
     cotangent,
 ):
-    vectors = jnp.concatenate(
-        [
-            query_bias,
-            value_bias,
-            out_bias,
-            down_bias,
-            first_gain,
-            first_shift,
-            second_gain,
-            second_shift,
-            up_bias,
-        ]
-    )
-    vectors = vectors.astype(F32).reshape(12, 1, 512)
-    places = slot_places[0]
-    starts = jnp.cumsum(lengths[0]) - lengths[0]
-    first = jnp.max(jnp.where(starts[None, :] <= places[:, None], starts[None, :], 0), axis=1)
-    query_info = jnp.zeros((8, places.shape[0]), jnp.int32).at[0].set(places).at[1].set(first)
-    key_info = jnp.broadcast_to(places[:, None], (places.shape[0], T))
+    vectors = (
+        query_bias,
+        value_bias,
+        out_bias,
+        down_bias,
+        first_gain,
+        first_shift,
+        second_gain,
+        second_shift,
+        up_bias,
+    )
     hbm = pl.BlockSpec(memory_space=pl.ANY)
     vmem = pl.BlockSpec(memory_space=pltpu.VMEM)
     outs = pl.pallas_call(
@@ -1151,10 +1267,10 @@
             jax.ShapeDtypeStruct((32, 1024), F32),
             jax.ShapeDtypeStruct((32, 4096), F32),
             jax.ShapeDtypeStruct((128, 1024), F32),
-            jax.ShapeDtypeStruct((16, 128), F32),
+            jax.ShapeDtypeStruct((40, 128), F32),
             jax.ShapeDtypeStruct((16, T, 1024), LOW),
         ),
-        in_specs=[vmem] * 5 + [hbm] * 4,
+        in_specs=[vmem] * 3 + [pl.BlockSpec(memory_space=pltpu.SMEM)] + [vmem] * 9 + [hbm] * 4,
         out_specs=(vmem,) * 7 + (hbm,),
         scratch_shapes=[scratch()],
         compiler_params=pltpu.CompilerParams(
@@ -1166,35 +1282,40 @@
     )(
         tokens[0],
         cotangent[0],
-        vectors,
-        key_info,
-        query_info,
+        slot_places,
+        lengths,
+        *vectors,
         in_weight,
         out_weight,
         up_weight,
         down_weight,
     )
-    layer_out, input_grad, in_grad, out_grad, up_grad, down_grad, vec = outs[:7]
-    index = lax.axis_index("ctx") * 2 + lax.axis_index("fsdp")
-    at = index % 4
-    small = lax.dynamic_slice(vec, (0, at * 32), (8, 32))
-    up_small = lax.dynamic_slice(vec, (8 + at, 0), (1, 128))[0]
+    small = [jax.ShapeDtypeStruct((32,), F32)] * 8 + [jax.ShapeDtypeStruct((T,), F32)]
+    outs = pl.pallas_call(
+        finish_kernel,
+        out_shape=[jax.ShapeDtypeStruct(one.shape, one.dtype) for one in outs[:6]] + small,
+        in_specs=[vmem] * 7,
+        out_specs=[vmem] * 15,
+    )(*outs[:7])
+    layer_out, input_grad, in_grad, out_grad, up_grad, down_grad = outs[:6]
+    query_sum, value_sum, out_sum, down_sum = outs[6:10]
+    gain_one, shift_one, gain_two, shift_two, up_sum = outs[10:]
     return (
         layer_out[None],
         input_grad[None],
         in_grad,
-        small[0],
-        small[1],
+        query_sum,
+        value_sum,
         out_grad,
-        small[2],
+        out_sum,
         up_grad,
-        up_small,
+        up_sum,
         down_grad,
-        small[3],
-        small[4],
-        small[5],
-        small[6],
-        small[7],
+        down_sum,
+        gain_one,
+        shift_one,
+        gain_two,
+        shift_two,
     )
 
 

time: 205 us -> 161 us (0.79)
  local copies, waits for them, and re-layouts: 24 us -> 0 us
  Pallas kernels: 177 us -> 160 us
  other arithmetic: 2.89 us -> 0 us
    pallas_call x1, Pallas kernels: 177 us -> 157 us  [body_fused(): pl.pallas_call(layer_kernel, out_shape=(jax.ShapeDtypeStruct((T, 1024), L...]
    unnamed x16 -> x0, local copies, waits for them, and re-layouts: 17.9 us -> none
    pallas_call x0 -> x1, Pallas kernels: none -> 2.93 us  [body_fused(): pl.pallas_call(finish_kernel, out_shape=[jax.ShapeDtypeStruct(one.shape,...]
where the time goes in v3:
time: 161 us
  Pallas kernels  160 us (99%)
    pallas_call x1, Pallas kernels, body_fused(): pl.pallas_call(layer_kernel, out_shape=(jax.ShapeDtypeStruct((T, 1024), L...  157 us

profile of v3, /device:TPU:0, one launch (start us, length us, event | category | flops | bytes accessed | tf_op | source)
XLA Modules:
  0.0 160.7 jit_solution(8267481495318127330)
XLA Ops:
  0.7 157.0 %shard_map.280 = (bf16[128,1024]{1,0:T(8,128)(2,1)}, bf16[128,1024]{1,0:T(8,128)(2,1)}, f32[32,3072]{1,0:T(8,128)}, f32[32,1024]{1,0:T(8,128)}, f32[32,4096]{1,0...) custom-call(bf16[128,1024]{1,0:T(8,128)(2,1)} %bitcast.4, ...), custom_call_target="tpu_custom_call" | custom-call | flops 16000000000 | bytes 41943040 | tf_op jit(solution)/shard_map/pallas_call | solution.py:1261
  157.6 2.9 %shard_map.281 = (bf16[128,1024]{1,0:T(8,128)(2,1)}, bf16[128,1024]{1,0:T(8,128)(2,1)}, f32[32,3072]{1,0:T(8,128)}, f32[32,1024]{1,0:T(8,128)}, f32[32,4096]{1,0...) custom-call(bf16[128,1024]{1,0:T(8,128)(2,1)} %get-tuple-element.37., ...), custom_call_target="tpu_custom_call" | custom-call | tf_op jit(solution)/shard_map/pallas_call | solution.py:1294

commit v4 on v3

--- a/solution.py
+++ b/solution.py
@@ -394,7 +394,7 @@
     send_qkv: Any
     qkv_t: Any
     kv: Any
-    scores: Any
+    pool: Any
     lse: Any
     delta: Any
     head_out: Any
@@ -416,12 +416,10 @@
     do_t: Any
     q_rows: Any
     do_rows: Any
-    down_mine: Any
     down_theirs: Any
     down_pair: Any
     down_line: Any
     up_mine: Any
-    up_theirs: Any
     up_pair: Any
     up_line: Any
     up_piece: Any
@@ -431,10 +429,13 @@
     out_line: Any
     dqkv: Any
     gp_t: Any
+    one_all: Any
+    col: Any
     in_mine: Any
-    in_theirs: Any
     in_pair: Any
-    in_send: Any
+    in_plane: Any
+    in_own: Any
+    in_line: Any
     in_recv: Any
     early_send: Any
     early_recv: Any
@@ -446,7 +447,9 @@
     sem_pair: Any
     sem_qkv: Any
     sem_one: Any
-    sem_relay: Any
+    sem_col: Any
+    sem_col_dq: Any
+    sem_in_plane: Any
     sem_cot: Any
     sem_head: Any
     sem_att: Any
@@ -461,7 +464,6 @@
     sem_late: Any
     sem_dq: Any
     sem_in_w: Any
-    sem_one_load: Any
 
 
 def scratch():
@@ -484,7 +486,7 @@
         send_qkv=v((16, 192, 128), LOW),
         qkv_t=v((192, 2048), LOW),
         kv=v((2048, 128), LOW),
-        scores=v((2048, 256), F32),
+        pool=v((512, 1024), F32),
         lse=v((1, 2048), F32),
         delta=v((1, 2048), F32),
         head_out=v((64, 2048), F32),
@@ -506,26 +508,27 @@
         do_t=v((64, 2048), LOW),
         q_rows=v((2048, 128), LOW),
         do_rows=v((2048, 128), LOW),
-        down_mine=v((4, 128, 1024), F32),
-        down_theirs=v((4, 128, 1024), LOW),
-        down_pair=v((4, 128, 1024), LOW),
+        down_theirs=v((512, 1024), LOW),
+        down_pair=v((512, 1024), LOW),
         down_line=v((3, 128, 1024), LOW),
-        up_mine=v((4, 128, 1024), F32),
-        up_theirs=v((4, 128, 1024), LOW),
-        up_pair=v((4, 128, 1024), LOW),
+        up_mine=v((512, 1024), F32),
+        up_pair=v((512, 1024), LOW),
         up_line=v((3, 128, 1024), LOW),
         up_piece=v((4, 32, 1024), F32),
-        out_mine=v((4, 32, 1024), F32),
-        out_theirs=v((4, 32, 1024), LOW),
-        out_pair=v((4, 32, 1024), LOW),
+        out_mine=v((128, 1024), F32),
+        out_theirs=v((128, 1024), LOW),
+        out_pair=v((128, 1024), LOW),
         out_line=v((3, 32, 1024), LOW),
         dqkv=v((16, 192, 128), LOW),
         gp_t=v((3072, 128), LOW),
-        in_mine=v((16, 48, 128), F32),
-        in_theirs=v((16, 48, 128), LOW),
-        in_pair=v((16, 48, 128), LOW),
-        in_send=v((16, 48, 128), LOW),
-        in_recv=v((16, 48, 128), LOW),
+        one_all=v((4, 128, 1024), LOW),
+        col=v((4, 4, 192, 128), LOW),
+        in_mine=v((4, 4, 32, 768), F32),
+        in_pair=v((512, 768), LOW),
+        in_plane=v((3, 128, 768), LOW),
+        in_own=v((4, 32, 768), F32),
+        in_line=v((3, 32, 768), LOW),
+        in_recv=v((4, 32, 768), LOW),
         early_send=v((8, 8, 128), F32),
         early_recv=v((16, 8, 128), F32),
         late_send=v((8, 8, 128), F32),
@@ -536,7 +539,9 @@
         sem_pair=sems(10),
         sem_qkv=sems(16),
         sem_one=sems(16),
-        sem_relay=sems(12),
+        sem_col=sems(16),
+        sem_col_dq=sems(16),
+        sem_in_plane=sems(3),
         sem_cot=sems(3),
         sem_head=sems(16),
         sem_att=sems(3),
@@ -551,7 +556,6 @@
         sem_late=sems(16),
         sem_dq=sems(16),
         sem_in_w=sems(12),
-        sem_one_load=pltpu.SemaphoreType.DMA((16,)),
     )
 
 
@@ -564,7 +568,7 @@
 ):
     vec_refs, rest = rest[:9], rest[9:]
     in_hbm, out_hbm, up_hbm, down_hbm = rest[:4]
-    layer_out, input_grad, in_out, out_out, up_out, down_out, vec_out, one_hbm, s = rest[4:]
+    layer_out, input_grad, in_out, out_out, up_out, down_out, vec_out, s = rest[4:]
     n = 16
     scale = HD ** (-0.5)
     c, f = lax.axis_index("ctx"), lax.axis_index("fsdp")
@@ -700,8 +704,7 @@
     for i in range(1, 4):
         loads[i].start()
         pairs[i].start()
-    keep = pltpu.make_async_copy(s.normed_one, one_hbm.at[c], s.sem_load.send.at[4])
-    keep.start()
+    s.one_all[z] = s.normed_one[...]
 
     place = place_ref[...]
     first, begun = jnp.zeros((1, 2048), jnp.int32), 0
@@ -721,21 +724,14 @@
 
     each_peer(qkv_arrived)
 
-    def one_copy(slot, sems, i, device):
-        return remote(one_hbm.at[slot], one_hbm.at[slot], Sems(sems.send, s.sem_one.recv), i, slot, device)
-
-    keep.wait()
     far_slot = far * 4 + p
-    one_far = one_copy(c, s.sem_one, 0, (far_slot, f))
+
+    def one_copy(slot, i, device):
+        return remote(s.one_all.at[slot], s.one_all.at[slot], s.sem_one, i, slot, device)
+
+    one_far = one_copy(z, 0, (far_slot, f))
     one_far.start()
     sent.append(one_far)
-
-    def relay(k, slot):
-        for i in range(3):
-            copy = one_copy(slot, s.sem_relay, k * 3 + i, planes[i])
-            copy.start()
-            sent.append(copy)
-
 
     for i in range(n):
         at = slice(i * T, i * T + T)
@@ -748,6 +744,9 @@
 
     def head_copy(dst):
         return remote(s.send_head.at[dst], s.att_t.at[p * 4 + z], s.sem_head, dst, c, (dst, f))
+
+    def score_at(k):
+        return s.pool.at[pl.ds(k // 4 * 256, 256), pl.ds(k % 4 * 256, 256)]
 
     def forward(i, carry):
         block = (c // 2 + i) % 8
@@ -757,14 +756,14 @@
         for k in range(8):
             keys = slice(k * 256, k * 256 + 256)
             score = jnp.where(seen(keys, at), dot(s.kv[keys], query), far_below)
-            s.scores[keys] = score
+            score_at(k)[...] = score
             top = jnp.maximum(top, jnp.max(score.reshape(32, 8, 256), axis=0))
         top = jnp.max(top, axis=0, keepdims=True)
         total = jnp.zeros((8, 256), F32)
         acc = jnp.zeros((64, 256), F32)
         for k in range(8):
             keys = slice(k * 256, k * 256 + 256)
-            grown = jnp.exp(s.scores[keys] - top)
+            grown = jnp.exp(score_at(k)[...] - top)
             total = total + jnp.sum(grown.reshape(32, 8, 256), axis=0)
             acc = acc + dot(s.qkv_t[128:192, keys], grown.astype(LOW))
         total = column_sum(total)
@@ -794,14 +793,15 @@
     each_peer(head_arrived)
 
     def one_arrived(slot):
-        one_copy(slot, s.sem_one, 0, (slot, f)).wait_recv()
-
-    one_arrived(far_slot)
+        one_copy(slot, 0, (far_slot, f)).wait_recv()
+
+    one_arrived(far)
     near_device = (near * 4 + p, f)
-    for i, slot in enumerate((c, far_slot)):
-        copy = one_copy(slot, s.sem_one, 1 + i, near_device)
+    for i, slot in enumerate((z, far)):
+        copy = one_copy(slot, 1 + i, near_device)
         copy.start()
         sent.append(copy)
+
     s.att_all[0] = s.att_t[pl.ds(p * 4, 4)]
     att_copies = to_planes(
         lambda i: s.att_t.at[pl.ds(plane_places[i] * 4, 4)], s.att_all, s.sem_att
@@ -889,12 +889,6 @@
         )
         return jnp.sum(recv[...], axis=0)
 
-    near_slots = (near * 4 + p, (near + 2) % 4 * 4 + p)
-    for slot in near_slots:
-        one_arrived(slot)
-    for k, slot in enumerate((c, far_slot) + near_slots):
-        relay(k, slot)
-
     for i in range(3):
         cot_copies[i].wait_recv()
         two_copies[i].wait_recv()
@@ -910,8 +904,8 @@
         grad_active = dot_nt(plane_rows(s.cot_all), s.down_full[at, :])
         s.grad_hidden[:, lanes(q, 256)] = (grad_active * slope).astype(LOW)
         part = dot_tn(active.astype(LOW), plane_rows(s.cot_all))
-        s.down_mine[q] = jnp.where(first_core, part[:T], part[T:])
-        s.down_theirs[q] = jnp.where(first_core, part[T:], part[:T]).astype(LOW)
+        s.pool[lanes(q, T)] = jnp.where(first_core, part[:T], part[T:])
+        s.down_theirs[lanes(q, T)] = jnp.where(first_core, part[T:], part[:T]).astype(LOW)
         return carry
 
     lax.fori_loop(0, 4, strip, 0)
@@ -924,46 +918,49 @@
         theirs = jnp.where(first_core, parts[:, 1], parts[:, 0])
         return mine, theirs.astype(LOW)
 
+    up_theirs = s.down_full.at[pl.ds(0, 512)]
+
     def up_rows(q, carry):
         left = s.two_all[:, :, lanes(q, 256)].reshape(512, 256)
         mine, theirs = split_rows(dot_tn(left, s.grad_hidden[...]))
-        s.up_mine[q] = mine.reshape(T, 1024)
-        s.up_theirs[q] = theirs.reshape(T, 1024)
+        s.up_mine[lanes(q, T)] = mine.reshape(T, 1024)
+        up_theirs[lanes(q, T)] = theirs.reshape(T, 1024)
         return carry
 
     lax.fori_loop(0, 4, up_rows, 0)
-    up_pair = remote(s.up_theirs, s.up_pair, s.sem_pair, 6, 6, sibling)
+    up_pair = remote(up_theirs, s.up_pair, s.sem_pair, 6, 6, sibling)
     up_pair.start()
 
     def to_near(mine, theirs, pair, line, base):
+        size = line.shape[1]
         copies = []
         for j in range(2):
-            at = (near + 2 * j) % 4
+            at = lanes((near + 2 * j) % 4, size)
             theirs[at] = (mine[at] + pair[at].astype(F32)).astype(LOW)
             copy = remote(
                 theirs.at[at], line.at[j], s.sem_line, base + j, base + j, (near * 4 + p, f)
             )
             copy.start()
             copies.append(copy)
-        for at in (z, far):
+        for at in (lanes(z, size), lanes(far, size)):
             mine[at] += pair[at].astype(F32)
         return copies
 
     def to_far(mine, theirs, line, base, copies):
+        size = line.shape[1]
         for copy in copies:
             copy.wait_recv()
-        mine[z] += line[0].astype(F32)
-        theirs[far] = (mine[far] + line[1].astype(F32)).astype(LOW)
-        copy = remote(
-            theirs.at[far], line.at[2], s.sem_line, base + 2, base + 2, (far_slot, f)
-        )
+        mine[lanes(z, size)] += line[0].astype(F32)
+        at = lanes(far, size)
+        theirs[at] = (mine[at] + line[1].astype(F32)).astype(LOW)
+        copy = remote(theirs.at[at], line.at[2], s.sem_line, base + 2, base + 2, (far_slot, f))
         copy.start()
         return copies + [copy]
 
     down_pair.wait()
-    down_line = to_near(s.down_mine, s.down_theirs, s.down_pair, s.down_line, 0)
+    down_line = to_near(s.pool, s.down_theirs, s.down_pair, s.down_line, 0)
     up_pair.wait()
-    up_line = to_near(s.up_mine, s.up_theirs, s.up_pair, s.up_line, 3)
+    up_line = to_near(s.up_mine, up_theirs, s.up_pair, s.up_line, 3)
     early_to = to_owners(s.early_grad, s.early_send, s.early_recv, s.sem_early)
 
     def qkv_done(dst):
@@ -1008,6 +1005,21 @@
             c,
             (dst, f),
         )
+
+    def col_copy(t, at, size, sems):
+        return remote(
+            s.send_qkv.at[t, pl.ds(at, size)],
+            s.col.at[p, t // 4, pl.ds(at, size)],
+            sems,
+            t,
+            p * 4 + t // 4,
+            (home + t % 4, f),
+        )
+
+    def each_column(step):
+        for k in range(1, 4):
+            for i in range(4):
+                step(i * 4 + (p + k) % 4)
 
     def backward(i, carry):
         block = (c // 2 + i) % 8
@@ -1035,16 +1047,23 @@
             def _():
                 grads_copy(dst).start()
 
+            @pl.when(dst % 4 != p)
+            def _():
+                col_copy(dst, 64, 128, s.sem_col).start()
+
         return carry
 
     lax.fori_loop(0, 4, backward, 0)
-    down_line = to_far(s.down_mine, s.down_theirs, s.down_line, 0, down_line)
+    down_line = to_far(s.pool, s.down_theirs, s.down_line, 0, down_line)
     lax.fori_loop(4, 8, backward, 0)
     for i in range(n):
         s.send_qkv[i, 0:64] = s.dq[:, i * T : i * T + T].astype(LOW)
+    each_column(lambda t: col_copy(t, 0, 64, s.sem_col_dq).start())
     each_peer(lambda dst: dq_copy(dst).start())
+    for i in range(4):
+        s.col[p, i] = s.send_qkv[i * 4 + p]
     s.dqkv[c] = s.send_qkv[c]
-    up_line = to_far(s.up_mine, s.up_theirs, s.up_line, 3, up_line)
+    up_line = to_far(s.up_mine, up_theirs, s.up_line, 3, up_line)
     for i in range(3):
         att_copies[i].wait_recv()
         branch_copies[i].wait_recv()
@@ -1052,44 +1071,43 @@
     for i in range(4):
         part = part + dot(s.att_all[i].reshape(256, T), s.branch_all[i])
     mine, theirs = split_rows(part)
-    s.out_mine[...] = mine
-    s.out_theirs[...] = theirs
+    s.out_mine[...] = mine.reshape(T, 1024)
+    s.out_theirs[...] = theirs.reshape(T, 1024)
     out_pair = remote(s.out_theirs, s.out_pair, s.sem_pair, 7, 7, sibling)
     out_pair.start()
     out_pair.wait()
     out_line = to_near(s.out_mine, s.out_theirs, s.out_pair, s.out_line, 6)
 
-    for k in range(4):
-        for i in range(3):
-            one_arrived((z + k) % 4 * 4 + plane_places[i])
-    one_loads = []
-    for i in range(n):
-        load = pltpu.make_async_copy(
-            one_hbm.at[i], s.down_full.at[pl.ds(i * T, T)], s.sem_one_load.at[i]
-        )
-        load.start()
-        one_loads.append(load)
-    for load in one_loads:
-        load.wait()
+    for slot in (near, (near + 2) % 4):
+        one_arrived(slot)
+    for at, size, sems in ((64, 128, s.sem_col), (0, 64, s.sem_col_dq)):
+        for k in range(1, 4):
+            for i in range(4):
+                q = (p + k) % 4
+                here = s.col.at[q, i, pl.ds(at, size)]
+                remote(here, here, sems, 0, q * 4 + i, (home + q, f)).wait_recv()
+    col_rows = s.up_full.at[pl.ds(0, 768), pl.ds(2048, 512)]
+    in_theirs = s.up_full.at[pl.ds(0, 512), pl.ds(0, 768)]
+    in_send = [s.up_full.at[pl.ds(i * T, T), pl.ds(1024, 768)] for i in range(3)]
+    for q in range(4):
+        for i in range(4):
+            for part in range(3):
+                col_rows[part * 256 + q * 64 : part * 256 + q * 64 + 64, i * T : i * T + T] = (
+                    s.col[q, i, part * 64 : part * 64 + 64]
+                )
     head_grad = jnp.concatenate([s.send_qkv[i] for i in range(n)], axis=1)
     bias_sums = dot_nt(jnp.ones((8, 2048), LOW), head_grad)
     s.vec_mine[16:24] = jnp.concatenate([bias_sums[:, 0:64] * scale, bias_sums[:, 128:192]], axis=1)
 
-    def packed(rows):
-        tail = jnp.concatenate([rows[:, 0:16, 128:192], rows[:, 16:32, 128:192]], axis=2)
-        return jnp.concatenate([rows[:, :, 0:128], tail], axis=1)
-
     for i in range(4):
-        part = dot(head_grad, s.down_full[0:2048, i * 256 : i * 256 + 256])
-        part = jnp.concatenate(
-            [part[0:64] * scale, part[64:192], jnp.zeros((64, 256), F32)], axis=0
-        )
-        for u in range(2):
-            parts = part[:, u * T : u * T + T].T.reshape(2, 2, 32, 256)
-            at = slice(4 * i + 2 * u, 4 * i + 2 * u + 2)
-            s.in_mine[at] = packed(jnp.where(first_core, parts[:, 0], parts[:, 1]))
-            s.in_theirs[at] = packed(jnp.where(first_core, parts[:, 1], parts[:, 0])).astype(LOW)
-    in_pair = remote(s.in_theirs, s.in_pair, s.sem_pair, 8, 8, sibling)
+        right = s.one_all[:, :, i * 256 : i * 256 + 256].reshape(512, 256)
+        part = dot(col_rows[...], right)
+        part = jnp.concatenate([part[0:256] * scale, part[256:768]], axis=0)
+        parts = part.T.reshape(4, 2, 32, 768)
+        s.in_mine[i] = jnp.where(first_core, parts[:, 0], parts[:, 1])
+        theirs = jnp.where(first_core, parts[:, 1], parts[:, 0])
+        in_theirs[i * T : i * T + T] = theirs.reshape(T, 768).astype(LOW)
+    in_pair = remote(in_theirs, s.in_pair, s.sem_pair, 8, 8, sibling)
     in_pair.start()
 
     def grads_arrived(src):
@@ -1112,14 +1130,6 @@
             (src, f),
         ).wait_recv()
 
-    in_pair.wait()
-    s.in_send[...] = (s.in_mine[...] + s.in_pair[...].astype(F32)).astype(LOW)
-
-    def in_copy(dst):
-        return remote(s.in_send.at[dst], s.in_recv.at[c], s.sem_in, dst, c, (dst, f))
-
-    each_peer(lambda dst: in_copy(dst).start())
-    s.in_recv[c] = s.in_send[c]
     each_peer(grads_arrived)
     for h in range(n):
         s.gp_t[1024 + h * 64 : 1088 + h * 64] = s.dqkv[h, 64:128]
@@ -1142,9 +1152,26 @@
         s.grad_middle[...] + standard_back(grad_one, row(4), unit_one, spread_one)
     ).astype(LOW)
 
+    in_pair.wait()
+
+    def in_total(q, at):
+        rows = pl.ds(pl.multiple_of(q * T + at * 32, 32), 32)
+        return s.in_mine[q, at] + s.in_pair[rows].astype(F32)
+
+    in_copies = []
+    for i in range(3):
+        for q in range(4):
+            at = plane_places[i]
+            in_send[i][q * 32 : q * 32 + 32] = in_total(q, at).astype(LOW)
+        copy = remote(in_send[i], s.in_plane.at[i], s.sem_in_plane, i, i, planes[i])
+        copy.start()
+        in_copies.append(copy)
+    for q in range(4):
+        s.in_own[q] = in_total(q, p)
+
     out_line = to_far(s.out_mine, s.out_theirs, s.out_line, 6, out_line)
     up_line[2].wait_recv()
-    up_sum = s.up_mine[z] + s.up_line[2].astype(F32)
+    up_sum = s.up_mine[lanes(z, T)] + s.up_line[2].astype(F32)
     s.up_piece[...] = up_sum.reshape(4, 32, 1024)
     up_copies = []
     for i in range(3):
@@ -1164,28 +1191,45 @@
             p, :, q * 256 : q * 256 + 256
         ]
     down_line[2].wait_recv()
-    down_out[...] = s.down_mine[z] + s.down_line[2].astype(F32)
+    down_out[...] = s.pool[lanes(z, T)] + s.down_line[2].astype(F32)
     out_line[2].wait_recv()
-    out_out[...] = s.out_mine[z] + s.out_line[2].astype(F32)
+    out_out[...] = s.out_mine[lanes(z, 32)] + s.out_line[2].astype(F32)
+
+    for copy in in_copies:
+        copy.wait_recv()
+    in_line = []
+    for k in range(1, 4):
+        at = (z + k) % 4
+        total = s.in_own[at]
+        for i in range(3):
+            total = total + s.in_plane[i, pl.ds(pl.multiple_of(at * 32, 32), 32)].astype(F32)
+        s.in_line[k - 1] = total.astype(LOW)
+        copy = remote(
+            s.in_line.at[k - 1], s.in_recv.at[z], s.sem_in, k - 1, z, (at * 4 + p, f)
+        )
+        copy.start()
+        in_line.append(copy)
+
+    def put_in(at, block):
+        for part in range(3):
+            columns = pl.ds(pl.multiple_of(part * 1024 + at * 256, 256), 256)
+            in_out[:, columns] = block[:, part * 256 : part * 256 + 256]
+
+    total = s.in_own[z]
+    for i in range(3):
+        total = total + s.in_plane[i, pl.ds(pl.multiple_of(z * 32, 32), 32)].astype(F32)
+    put_in(z, total)
 
     s.vec_mine[0:8] = from_owners(s.early_send, s.early_recv, s.sem_early)
     s.vec_mine[8:16] = from_owners(s.late_send, s.late_recv, s.sem_late)
     vec_pair = remote(s.vec_mine, s.vec_pair, s.sem_pair, 9, 9, sibling)
     vec_pair.start()
 
-    def in_arrived(src):
-        remote(s.in_send.at[src], s.in_recv.at[src], s.sem_in, src, src, (src, f)).wait_recv()
-
-    each_peer(in_arrived)
-    for i in range(8):
-        a, b = s.in_recv[2 * i].astype(F32), s.in_recv[2 * i + 1].astype(F32)
-        at = i * T
-        in_out[:, at : at + T] = jnp.concatenate([a[0:32, 0:64], b[0:32, 0:64]], axis=1)
-        at = 1024 + i * T
-        in_out[:, at : at + T] = jnp.concatenate([a[0:32, 64:T], b[0:32, 64:T]], axis=1)
-        at = 2048 + i * T
-        in_out[0:16, at : at + T] = jnp.concatenate([a[32:48, 0:64], b[32:48, 0:64]], axis=1)
-        in_out[16:32, at : at + T] = jnp.concatenate([a[32:48, 64:T], b[32:48, 64:T]], axis=1)
+    for k in range(1, 4):
+        at = (z + k) % 4
+        here = s.in_recv.at[at]
+        remote(here, here, s.sem_in, 0, at, (at * 4 + p, f)).wait_recv()
+        put_in(at, s.in_recv[at].astype(F32))
     vec_pair.wait()
     total = s.vec_mine[...] + s.vec_pair[...]
     place = (c * 2 + f) % 4
@@ -1203,6 +1247,9 @@
         for part in range(3):
             in_copy_of(g, part).wait_send()
     sent += [copy for line in (down_line, up_line, out_line) for copy in line]
+    sent += in_copies + in_line
+    each_column(lambda t: col_copy(t, 64, 128, s.sem_col).wait_send())
+    each_column(lambda t: col_copy(t, 0, 64, s.sem_col_dq).wait_send())
     for copy in sent:
         copy.wait_send()
 
@@ -1210,7 +1257,6 @@
         back_copy(dst).wait_send()
         grads_copy(dst).wait_send()
         dq_copy(dst).wait_send()
-        in_copy(dst).wait_send()
         early_to(dst).wait_send()
         late_to(dst).wait_send()
 
@@ -1268,13 +1314,12 @@
             jax.ShapeDtypeStruct((32, 4096), F32),
             jax.ShapeDtypeStruct((128, 1024), F32),
             jax.ShapeDtypeStruct((40, 128), F32),
-            jax.ShapeDtypeStruct((16, T, 1024), LOW),
         ),
         in_specs=[vmem] * 3 + [pl.BlockSpec(memory_space=pltpu.SMEM)] + [vmem] * 9 + [hbm] * 4,
-        out_specs=(vmem,) * 7 + (hbm,),
+        out_specs=(vmem,) * 7,
         scratch_shapes=[scratch()],
         compiler_params=pltpu.CompilerParams(
-            collective_id=0, has_side_effects=True, vmem_limit_bytes=60 * 2**20
+            collective_id=0, has_side_effects=True, vmem_limit_bytes=59 * 2**20
         ),
         cost_estimate=pl.CostEstimate(
             flops=16 * 10**9, bytes_accessed=40 * 2**20, transcendentals=10**7

time: 161 us -> 151 us (0.938)
  Pallas kernels: 160 us -> 150 us
    pallas_call x1, Pallas kernels: 157 us -> 147 us  [body_fused(): pl.pallas_call(layer_kernel, out_shape=(jax.ShapeDtypeStruct((T, 1024), L...]
where the time goes in v4:
time: 151 us
  Pallas kernels  150 us (99%)
    pallas_call x1, Pallas kernels, body_fused(): pl.pallas_call(layer_kernel, out_shape=(jax.ShapeDtypeStruct((T, 1024), L...  147 us

profile of v4, /device:TPU:0, one launch (start us, length us, event | category | flops | bytes accessed | tf_op | source)
XLA Modules:
  0.0 151.0 jit_solution(5994473792886210626)
XLA Ops:
  0.7 147.3 %shard_map.280 = (bf16[128,1024]{1,0:T(8,128)(2,1)}, bf16[128,1024]{1,0:T(8,128)(2,1)}, f32[32,3072]{1,0:T(8,128)}, f32[32,1024]{1,0:T(8,128)}, f32[32,4096]{1,0...) custom-call(bf16[128,1024]{1,0:T(8,128)(2,1)} %bitcast.4, bf16[128,1024]{1,0:T(8,128)(2,1)} %bitcast.5, ...), custom_call_target="tpu_custom_call" | custom-call | flops 16000000000 | bytes 41943040 | tf_op jit(solution)/shard_map/pallas_call | solution.py:1307
  147.9 2.9 %shard_map.281 = (bf16[128,1024]{1,0:T(8,128)(2,1)}, bf16[128,1024]{1,0:T(8,128)(2,1)}, f32[32,3072]{1,0:T(8,128)}, f32[32,1024]{1,0:T(8,128)}, f32[32,4096]{1,0...) custom-call(bf16[128,1024]{1,0:T(8,128)(2,1)} %get-tuple-element.37., ...), custom_call_target="tpu_custom_call" | custom-call | tf_op jit(solution)/shard_map/pallas_call | solution.py:1339

commit v5 on v4

--- a/solution.py
+++ b/solution.py
@@ -447,6 +447,8 @@
     sem_pair: Any
     sem_qkv: Any
     sem_one: Any
+    sem_down_pair: Any
+    sem_up_pair: Any
     sem_col: Any
     sem_col_dq: Any
     sem_in_plane: Any
@@ -539,6 +541,8 @@
         sem_pair=sems(10),
         sem_qkv=sems(16),
         sem_one=sems(16),
+        sem_down_pair=sems(4),
+        sem_up_pair=sems(4),
         sem_col=sems(16),
         sem_col_dq=sems(16),
         sem_in_plane=sems(3),
@@ -620,6 +624,7 @@
         s.vec[f, 8 + i] = vec_refs[8][i * 512 : i * 512 + 512].astype(F32).reshape(1, 512)
     in_load = pltpu.make_async_copy(in_hbm, s.in_full.at[pl.ds(f * 512, 512)], s.sem_load.send.at[0])
     in_load.start()
+    unit_one, unused = standard(tok_ref[...].astype(F32))
     pl.semaphore_wait(barrier, n)
     vec_copy = remote(s.vec.at[f], s.vec.at[f], s.sem_pair, 4, 4, sibling)
     vec_copy.start()
@@ -658,7 +663,6 @@
     def row(i):
         return jnp.concatenate([s.vec[0, i], s.vec[1, i]], axis=1)
 
-    unit_one, unused = standard(tok_ref[...].astype(F32))
     s.cot_all[0] = cot_ref[...]
     vec_copy.wait_recv()
     s.normed_one[...] = (unit_one * row(4) + row(5)).astype(LOW)
@@ -803,10 +807,6 @@
         sent.append(copy)
 
     s.att_all[0] = s.att_t[pl.ds(p * 4, 4)]
-    att_copies = to_planes(
-        lambda i: s.att_t.at[pl.ds(plane_places[i] * 4, 4)], s.att_all, s.sem_att
-    )
-    sent += att_copies
     for i in range(8):
         slots = [(h % 4) * 4 + h // 4 for h in (2 * i, 2 * i + 1)]
         block = jnp.concatenate([s.att_t[slots[0]], s.att_t[slots[1]]], axis=0)
@@ -870,6 +870,10 @@
     s.do_t[:, lanes(c, T)] = s.send_head[c]
     branch_copies = to_planes(lambda i: s.branch_all.at[0], s.branch_all, s.sem_branch)
     sent += branch_copies
+    att_copies = to_planes(
+        lambda i: s.att_t.at[pl.ds(plane_places[i] * 4, 4)], s.att_all, s.sem_att
+    )
+    sent += att_copies
 
     def to_owners(grad, send, recv, sems):
         def copy_to(dst):
@@ -896,7 +900,15 @@
     def plane_rows(ref):
         return ref[...].reshape(512, 1024)
 
-    def strip(q, carry):
+    def block_of(i):
+        return (near + (z - near) * (i // 2) + 2 * (i % 2)) % 4
+
+    def pair_copy(theirs, pair, sems, i):
+        at = lanes(block_of(i), T)
+        return remote(theirs.at[at], pair.at[at], sems, i, i, sibling)
+
+    def strip(i, carry):
+        q = block_of(i)
         at = pl.ds(pl.multiple_of(q * 1024 + p * 256, 256), 256)
         shift = s.vec[q // 2, 8 + (q % 2) * 2 + p // 2, :, lanes(p % 2, 256)]
         hidden = dot(plane_rows(s.two_all), s.up_full[:, at]) + shift
@@ -906,35 +918,14 @@
         part = dot_tn(active.astype(LOW), plane_rows(s.cot_all))
         s.pool[lanes(q, T)] = jnp.where(first_core, part[:T], part[T:])
         s.down_theirs[lanes(q, T)] = jnp.where(first_core, part[T:], part[:T]).astype(LOW)
+        pair_copy(s.down_theirs, s.down_pair, s.sem_down_pair, i).start()
         return carry
 
-    lax.fori_loop(0, 4, strip, 0)
-    down_pair = remote(s.down_theirs, s.down_pair, s.sem_pair, 5, 5, sibling)
-    down_pair.start()
-
-    def split_rows(part):
-        parts = part.reshape(4, 2, 32, 1024)
-        mine = jnp.where(first_core, parts[:, 0], parts[:, 1])
-        theirs = jnp.where(first_core, parts[:, 1], parts[:, 0])
-        return mine, theirs.astype(LOW)
-
-    up_theirs = s.down_full.at[pl.ds(0, 512)]
-
-    def up_rows(q, carry):
-        left = s.two_all[:, :, lanes(q, 256)].reshape(512, 256)
-        mine, theirs = split_rows(dot_tn(left, s.grad_hidden[...]))
-        s.up_mine[lanes(q, T)] = mine.reshape(T, 1024)
-        up_theirs[lanes(q, T)] = theirs.reshape(T, 1024)
-        return carry
-
-    lax.fori_loop(0, 4, up_rows, 0)
-    up_pair = remote(up_theirs, s.up_pair, s.sem_pair, 6, 6, sibling)
-    up_pair.start()
-
-    def to_near(mine, theirs, pair, line, base):
+    def to_near(mine, theirs, pair, line, base, ready):
         size = line.shape[1]
         copies = []
         for j in range(2):
+            ready(j)
             at = lanes((near + 2 * j) % 4, size)
             theirs[at] = (mine[at] + pair[at].astype(F32)).astype(LOW)
             copy = remote(
@@ -942,26 +933,50 @@
             )
             copy.start()
             copies.append(copy)
-        for at in (lanes(z, size), lanes(far, size)):
-            mine[at] += pair[at].astype(F32)
         return copies
 
-    def to_far(mine, theirs, line, base, copies):
+    def to_far(mine, theirs, pair, line, base, ready, copies):
         size = line.shape[1]
+        for j in (2, 3):
+            ready(j)
         for copy in copies:
             copy.wait_recv()
-        mine[lanes(z, size)] += line[0].astype(F32)
+        at = lanes(z, size)
+        mine[at] += pair[at].astype(F32) + line[0].astype(F32)
         at = lanes(far, size)
-        theirs[at] = (mine[at] + line[1].astype(F32)).astype(LOW)
+        theirs[at] = (mine[at] + (pair[at].astype(F32) + line[1].astype(F32))).astype(LOW)
         copy = remote(theirs.at[at], line.at[2], s.sem_line, base + 2, base + 2, (far_slot, f))
         copy.start()
         return copies + [copy]
 
-    down_pair.wait()
-    down_line = to_near(s.pool, s.down_theirs, s.down_pair, s.down_line, 0)
-    up_pair.wait()
-    up_line = to_near(s.up_mine, up_theirs, s.up_pair, s.up_line, 3)
-    early_to = to_owners(s.early_grad, s.early_send, s.early_recv, s.sem_early)
+    up_theirs = s.down_full.at[pl.ds(0, 512)]
+
+    def down_ready(i):
+        pair_copy(s.down_theirs, s.down_pair, s.sem_down_pair, i).wait()
+
+    def up_ready(i):
+        pair_copy(up_theirs, s.up_pair, s.sem_up_pair, i).wait()
+
+    lax.fori_loop(0, 4, strip, 0)
+    down_line = to_near(s.pool, s.down_theirs, s.down_pair, s.down_line, 0, down_ready)
+
+    def split_rows(part):
+        parts = part.reshape(4, 2, 32, 1024)
+        mine = jnp.where(first_core, parts[:, 0], parts[:, 1])
+        theirs = jnp.where(first_core, parts[:, 1], parts[:, 0])
+        return mine, theirs.astype(LOW)
+
+    def up_rows(i, carry):
+        q = block_of(i)
+        left = s.two_all[:, :, lanes(q, 256)].reshape(512, 256)
+        mine, theirs = split_rows(dot_tn(left, s.grad_hidden[...]))
+        s.up_mine[lanes(q, T)] = mine.reshape(T, 1024)
+        up_theirs[lanes(q, T)] = theirs.reshape(T, 1024)
+        pair_copy(up_theirs, s.up_pair, s.sem_up_pair, i).start()
+        return carry
+
+    lax.fori_loop(0, 4, up_rows, 0)
+
 
     def qkv_done(dst):
         qkv_copy(dst).wait_send()
@@ -986,6 +1001,8 @@
     s.delta[...] = column_sum(s.do_t[...].astype(F32) * s.head_out[...])
     s.dq[...] = jnp.zeros((64, 2048), F32)
 
+    up_line = to_near(s.up_mine, up_theirs, s.up_pair, s.up_line, 3, up_ready)
+    early_to = to_owners(s.early_grad, s.early_send, s.early_recv, s.sem_early)
     def grads_copy(dst):
         return remote(
             s.send_qkv.at[dst, pl.ds(64, 128)],
@@ -1053,9 +1070,9 @@
 
         return carry
 
-    lax.fori_loop(0, 4, backward, 0)
-    down_line = to_far(s.pool, s.down_theirs, s.down_line, 0, down_line)
-    lax.fori_loop(4, 8, backward, 0)
+    lax.fori_loop(0, 6, backward, 0)
+    down_line = to_far(s.pool, s.down_theirs, s.down_pair, s.down_line, 0, down_ready, down_line)
+    lax.fori_loop(6, 8, backward, 0)
     for i in range(n):
         s.send_qkv[i, 0:64] = s.dq[:, i * T : i * T + T].astype(LOW)
     each_column(lambda t: col_copy(t, 0, 64, s.sem_col_dq).start())
@@ -1063,7 +1080,7 @@
     for i in range(4):
         s.col[p, i] = s.send_qkv[i * 4 + p]
     s.dqkv[c] = s.send_qkv[c]
-    up_line = to_far(s.up_mine, up_theirs, s.up_line, 3, up_line)
+    up_line = to_far(s.up_mine, up_theirs, s.up_pair, s.up_line, 3, up_ready, up_line)
     for i in range(3):
         att_copies[i].wait_recv()
         branch_copies[i].wait_recv()
@@ -1076,7 +1093,9 @@
     out_pair = remote(s.out_theirs, s.out_pair, s.sem_pair, 7, 7, sibling)
     out_pair.start()
     out_pair.wait()
-    out_line = to_near(s.out_mine, s.out_theirs, s.out_pair, s.out_line, 6)
+    out_line = to_near(
+        s.out_mine, s.out_theirs, s.out_pair, s.out_line, 6, lambda i: None
+    )
 
     for slot in (near, (near + 2) % 4):
         one_arrived(slot)
@@ -1169,7 +1188,7 @@
     for q in range(4):
         s.in_own[q] = in_total(q, p)
 
-    out_line = to_far(s.out_mine, s.out_theirs, s.out_line, 6, out_line)
+    out_line = to_far(s.out_mine, s.out_theirs, s.out_pair, s.out_line, 6, lambda i: None, out_line)
     up_line[2].wait_recv()
     up_sum = s.up_mine[lanes(z, T)] + s.up_line[2].astype(F32)
     s.up_piece[...] = up_sum.reshape(4, 32, 1024)

time: 151 us -> 145 us (0.960)
  Pallas kernels: 150 us -> 144 us
    pallas_call x1, Pallas kernels: 147 us -> 141 us  [body_fused(): pl.pallas_call(layer_kernel, out_shape=(jax.ShapeDtypeStruct((T, 1024), L...]
where the time goes in v5:
time: 145 us; the launch traced here: 144 us
  Pallas kernels  144 us (99%)
    pallas_call x1, Pallas kernels, body_fused(): pl.pallas_call(layer_kernel, out_shape=(jax.ShapeDtypeStruct((T, 1024), L...  141 us
    pallas_call x1, Pallas kernels, body_fused(): pl.pallas_call(finish_kernel, out_shape=[jax.ShapeDtypeStruct(one.shape,...  2.93 us

profile of v5, /device:TPU:0, one launch (start us, length us, event | category | flops | bytes accessed | tf_op | source)
XLA Modules:
  0.0 144.5 jit_solution(10934720804267391089)
XLA Ops:
  0.7 140.7 %shard_map.280 = (bf16[128,1024]{1,0:T(8,128)(2,1)}, bf16[128,1024]{1,0:T(8,128)(2,1)}, f32[32,3072]{1,0:T(8,128)}, f32[32,1024]{1,0:T(8,128)}, f32[32,4096]{1,0...) custom-call(bf16[128,1024]{1,0:T(8,128)(2,1)} %bitcast.4, bf16[128,1024]{1,0:T(8,128)(2,1)} %bitcast.5, ...), custom_call_target="tpu_custom_call" | custom-call | flops 16000000000 | bytes 41943040 | tf_op jit(solution)/shard_map/pallas_call | solution.py:1326
  141.4 2.9 %shard_map.281 = (bf16[128,1024]{1,0:T(8,128)(2,1)}, bf16[128,1024]{1,0:T(8,128)(2,1)}, f32[32,3072]{1,0:T(8,128)}, f32[32,1024]{1,0:T(8,128)}, f32[32,4096]{1,0...) custom-call(bf16[128,1024]{1,0:T(8,128)(2,1)} %get-tuple-element.37., ...), custom_call_target="tpu_custom_call" | custom-call | tf_op jit(solution)/shard_map/pallas_call | solution.py:1358

commit v6 on v5

--- a/solution.py
+++ b/solution.py
@@ -1080,22 +1080,6 @@
     for i in range(4):
         s.col[p, i] = s.send_qkv[i * 4 + p]
     s.dqkv[c] = s.send_qkv[c]
-    up_line = to_far(s.up_mine, up_theirs, s.up_pair, s.up_line, 3, up_ready, up_line)
-    for i in range(3):
-        att_copies[i].wait_recv()
-        branch_copies[i].wait_recv()
-    part = jnp.zeros((256, 1024), F32)
-    for i in range(4):
-        part = part + dot(s.att_all[i].reshape(256, T), s.branch_all[i])
-    mine, theirs = split_rows(part)
-    s.out_mine[...] = mine.reshape(T, 1024)
-    s.out_theirs[...] = theirs.reshape(T, 1024)
-    out_pair = remote(s.out_theirs, s.out_pair, s.sem_pair, 7, 7, sibling)
-    out_pair.start()
-    out_pair.wait()
-    out_line = to_near(
-        s.out_mine, s.out_theirs, s.out_pair, s.out_line, 6, lambda i: None
-    )
 
     for slot in (near, (near + 2) % 4):
         one_arrived(slot)
@@ -1128,6 +1112,23 @@
         in_theirs[i * T : i * T + T] = theirs.reshape(T, 768).astype(LOW)
     in_pair = remote(in_theirs, s.in_pair, s.sem_pair, 8, 8, sibling)
     in_pair.start()
+    up_line = to_far(s.up_mine, up_theirs, s.up_pair, s.up_line, 3, up_ready, up_line)
+    for i in range(3):
+        att_copies[i].wait_recv()
+        branch_copies[i].wait_recv()
+    part = jnp.zeros((256, 1024), F32)
+    for i in range(4):
+        part = part + dot(s.att_all[i].reshape(256, T), s.branch_all[i])
+    mine, theirs = split_rows(part)
+    s.out_mine[...] = mine.reshape(T, 1024)
+    s.out_theirs[...] = theirs.reshape(T, 1024)
+    out_pair = remote(s.out_theirs, s.out_pair, s.sem_pair, 7, 7, sibling)
+    out_pair.start()
+    out_pair.wait()
+    out_line = to_near(
+        s.out_mine, s.out_theirs, s.out_pair, s.out_line, 6, lambda i: None
+    )
+
 
     def grads_arrived(src):
         remote(

time: 145 us -> 144 us (level)
  no operation moved by 1% of the time
where the time goes in v6:
time: 144 us
  Pallas kernels  143 us (99%)
    pallas_call x1, Pallas kernels, body_fused(): pl.pallas_call(layer_kernel, out_shape=(jax.ShapeDtypeStruct((T, 1024), L...  140 us
    pallas_call x1, Pallas kernels, body_fused(): pl.pallas_call(finish_kernel, out_shape=[jax.ShapeDtypeStruct(one.shape,...  2.93 us

profile of v6, /device:TPU:0, one launch (start us, length us, event | category | flops | bytes accessed | tf_op | source)
XLA Modules:
  0.0 143.8 jit_solution(15188124359343439412)
XLA Ops:
  0.7 140.0 %shard_map.280 = (bf16[128,1024]{1,0:T(8,128)(2,1)}, bf16[128,1024]{1,0:T(8,128)(2,1)}, f32[32,3072]{1,0:T(8,128)}, f32[32,1024]{1,0:T(8,128)}, f32[32,4096]{1,0...) custom-call(bf16[128,1024]{1,0:T(8,128)(2,1)} %bitcast.4, bf16[128,1024]{1,0:T(8,128)(2,1)} %bitcast.5, ...), custom_call_target="tpu_custom_call" | custom-call | flops 16000000000 | bytes 41943040 | tf_op jit(solution)/shard_map/pallas_call | solution.py:1327
  140.7 2.9 %shard_map.281 = (bf16[128,1024]{1,0:T(8,128)(2,1)}, bf16[128,1024]{1,0:T(8,128)(2,1)}, f32[32,3072]{1,0:T(8,128)}, f32[32,1024]{1,0:T(8,128)}, f32[32,4096]{1,0...) custom-call(bf16[128,1024]{1,0:T(8,128)(2,1)} %get-tuple-element.37., ...), custom_call_target="tpu_custom_call" | custom-call | tf_op jit(solution)/shard_map/pallas_call | solution.py:1359
